TPU v7x, 32 devices: a whole 2x2x4 slice. The times are simulated.
32 devices in a mesh: row: 8 (over z, core), col: 4 (over y, x).
Axes of the slice: x: 2, y: 2, z: 4, core: 2. Of those that a mesh axis runs over, the one named last changes fastest.
Arguments:
- query: bfloat16 [192, 1024, 128], P('row', 'col'), may hold values from -12 to 12
- key: bfloat16 [192, 1024, 128], P('row', 'col'), may hold values from -6 to 6
- value: bfloat16 [192, 1024, 128], P('row', 'col'), may hold values from -6 to 6
- gate: bfloat16 [192, 1024, 128], P('row', 'col'), may hold values from -6 to 6
- d_out: bfloat16 [192, 1024, 128], P('row', 'col'), may hold values from -6 to 6
- bias: bfloat16 [4, 1024, 1024], P(None, 'col'), may hold values from -6 to 6
- length: int32 [1], replicated, may hold values from 513 to 1024
Outputs:
- d_query: bfloat16 [192, 1024, 128], P('row', 'col')
- d_key: bfloat16 [192, 1024, 128], P('row', 'col')
- d_value: bfloat16 [192, 1024, 128], P('row', 'col')
- d_gate: bfloat16 [192, 1024, 128], P('row', 'col')
- d_bias: float32 [4, 1024, 1024], P(None, 'row', 'col')
All inputs are finite; a program needn't handle non-finite values.
Results may differ from a plain program's by a relative error of at most 0.014.
Values may be sent and summed in bfloat16 or wider, within the bound.
No kernel may reach another device: no remote copies, remote signals or barrier semaphores. Data moves between devices by JAX's collectives and lax.ppermute only.
A program may use at most 128 MiB of HBM per device.

v0:
```python
import functools
import itertools

import jax
import jax.numpy as jnp
from jax import lax
from jax.experimental import pallas as pl
from jax.experimental.pallas import tpu as pltpu
from jax.sharding import PartitionSpec as P

LOG2E = 1.4426950408889634
MASKED = -1e30
SHARES = (1, 2, 4, 5)
INWARD = ((0,), (1,), (2,), (3,))
OUTWARD = ((0, 1, 2), (3,))
PIECES = 4


def dot(a, b, dims):
    return lax.dot_general(a, b, (dims, ((), ())), preferred_element_type=jnp.float32)


def peer_of(me, step):
    return jnp.bitwise_xor(me, step)


def pack_kernel(heads, groups, with_bias, info, q_ref, k_ref, v_ref, g_ref, o_ref, *refs):
    n_col = heads * groups
    outs, turned = refs[-1 - n_col : -1], refs[-1]
    me = info[1]
    count, _, channels = q_ref.shape[1:]
    c = channels // heads
    lines = count * PIECES * c
    for i in range(count):
        for g in range(groups):
            gated = o_ref[g, i].astype(jnp.float32) * jax.nn.sigmoid(g_ref[g, i].astype(jnp.float32))
            pieces = (q_ref[g, i], k_ref[g, i], v_ref[g, i], gated.astype(jnp.bfloat16))
            for piece, x in enumerate(pieces):
                turned[g, i, piece] = x.T
        for step in range(n_col):
            peer = peer_of(me, step)
            head = pl.multiple_of(peer // groups * c, c)
            base = outs[step].shape[0] - lines
            for piece in range(PIECES):
                at = base + (i * PIECES + piece) * c
                outs[step][at : at + c, :] = turned[peer % groups, i, piece, pl.ds(head, c), :]
    if with_bias:
        for step in range(n_col):
            base = outs[step].shape[0] - lines
            keys = pl.ds(pl.multiple_of(info[2] * base, base), base) if step else slice(None)
            outs[step][:base, :] = refs[0][peer_of(me, step) // groups, :, keys].T


def unpack_kernel(heads, groups, info, g_ref, o_ref, *refs):
    n_col = heads * groups
    ins, (dq, dk, dv, dg, token, whole) = refs[:n_col], refs[-6:]
    token[...] = jnp.zeros_like(token)
    me = info[1]
    count, _, channels = g_ref.shape[1:]
    c = channels // heads
    for i in range(count):
        for step in range(n_col):
            peer = peer_of(me, step)
            head = pl.multiple_of(peer // groups * c, c)
            for piece in range(PIECES):
                at = (i * PIECES + piece) * c
                whole[peer % groups, i, piece, pl.ds(head, c), :] = ins[step][at : at + c, :]
        for g in range(groups):
            dq[g, i] = whole[g, i, 0].T
            dk[g, i] = whole[g, i, 1].T
            dv[g, i] = whole[g, i, 2].T
            attended = whole[g, i, 3].T.astype(jnp.float32)
            s = jax.nn.sigmoid(g_ref[g, i].astype(jnp.float32))
            dg[g, i] = (o_ref[g, i].astype(jnp.float32) * attended * s * (1.0 - s)).astype(jnp.bfloat16)


def woven(*queues):
    order = [(at / len(q), which, at) for which, q in enumerate(queues) for at in range(len(q))]
    for _, which, at in sorted(order):
        queues[which][at]()


def attention_kernel(n_col, together, c, scaling, first, last, info, *refs):
    bias_in, ins, refs = refs[: 2 * n_col - 1], refs[2 * n_col - 1 : 3 * n_col - 1], refs[3 * n_col - 1 :]
    scratch, refs = refs[-14:], refs[:-14]
    bias, total_s, q_s, g_s, k_s, v_s, k_turned, v_turned, dq_s, at_s, dkv, logits, weights, grads = scratch
    if not first:
        total_in = refs[0]
    *totals, token = refs[-3:] if last else refs[-2:]
    outs = refs[-n_col - len(totals) - 1 : -len(totals) - 1]
    total = total_s if last else totals[0]
    length, me, side, level = info[0], info[1], info[2], info[3]
    blk = ins[0].shape[1]
    n = n_col * blk
    tile = min(256, n)
    tiles = range(0, n, tile)
    deep = k_s.shape[1]
    some = range(together)

    @pl.when(pl.program_id(0) == 0)
    def _():
        token[...] = jnp.zeros_like(token)
        if first:
            total[...] = jnp.zeros_like(total)
        else:
            total[...] = total_in[...]
        half = n // 2
        bias[me] = bias_in[0][...].astype(jnp.float32) * LOG2E
        for step in range(1, n_col):
            for table, which in ((bias_in[step], side), (bias_in[n_col + step - 1], 1 - side)):
                keys = pl.ds(pl.multiple_of(which * half, half), half)
                bias[peer_of(me, step), keys, :] = table[...].astype(jnp.float32) * LOG2E
        rows = lax.broadcasted_iota(jnp.int32, (deep - 2 * c, n), 0)
        keys = lax.broadcasted_iota(jnp.int32, (deep - 2 * c, n), 1)
        mask = jnp.logical_and(rows == 0, keys >= length)
        for r in some:
            k_s[r, 2 * c :, :] = jnp.where(mask, MASKED, 0.0).astype(jnp.bfloat16)
            v_s[r, c:, :] = jnp.ones((deep - c, n), jnp.bfloat16)
            q_s[r, :, 2 * c :, :] = jnp.ones((n_col, deep - 2 * c, blk), jnp.bfloat16)

    def rows_of(r, piece):
        at = (r * PIECES + piece) * c
        return slice(at, at + c)

    for r in some:
        for step in range(n_col):
            jb = peer_of(me, step)
            span = pl.ds(pl.multiple_of(jb * blk, blk), blk)
            q = ins[step][rows_of(r, 0), :].astype(jnp.float32) * (scaling * LOG2E)
            high = q.astype(jnp.bfloat16)
            q_s[r, jb, :c, :] = high
            q_s[r, jb, c : 2 * c, :] = (q - high.astype(jnp.float32)).astype(jnp.bfloat16)
            k = ins[step][rows_of(r, 1), :]
            k_s[r, :c, span] = k
            k_s[r, c : 2 * c, span] = k
            v_s[r, :c, span] = ins[step][rows_of(r, 2), :]
            g_s[r, jb] = ins[step][rows_of(r, 3), :]
    for r in some:
        k_turned[r] = k_s[r].T
        v_turned[r] = v_s[r].T
    tops, scaled, scales = {}, {}, {}

    def score(jb, r, t):
        part = dot(k_turned[r, t : t + tile, :], q_s[r, jb], ((1,), (0,))) + bias[jb, t : t + tile, :]
        logits[jb % 2, r, t : t + tile, :] = part
        top = jnp.max(part.reshape(tile // 8, 8, blk), axis=0)
        tops[jb, r] = jnp.maximum(tops[jb, r], top) if t else top

    def expand(jb, r, t):
        if t == 0:
            tops[jb, r] = jnp.max(tops[jb, r], axis=0, keepdims=True)
        part = jnp.exp2(logits[jb % 2, r, t : t + tile, :] - tops[jb, r])
        weights[jb % 2, r, t : t + tile, :] = part.astype(jnp.bfloat16)

    def attend(jb, r):
        summed = dot(v_s[r, : c + 16, :], weights[jb % 2, r], ((1,), (0,)))
        inverse = 1.0 / summed[c : c + 1, :]
        attended = summed[:c, :] * inverse
        at_s[r, jb] = attended.astype(jnp.bfloat16)
        g = g_s[r, jb].astype(jnp.float32)
        row_dot = jnp.sum(g * attended, axis=0, keepdims=True) * (-inverse)
        high = row_dot.astype(jnp.bfloat16).astype(jnp.float32)
        rows = lax.broadcasted_iota(jnp.int32, (deep - c, blk), 0)
        tail = jnp.where(rows == 0, high, jnp.where(rows == 1, row_dot - high, 0.0))
        scaled[jb, r] = (g * inverse).astype(jnp.bfloat16)
        scales[jb, r] = jnp.concatenate([scaled[jb, r], tail.astype(jnp.bfloat16)], axis=0)

    def back(jb, t):
        added = total[jb, t : t + tile, :]
        for r in some:
            grad = dot(v_turned[r, t : t + tile, :], scales[jb, r], ((1,), (0,)))
            grad = grad * weights[jb % 2, r, t : t + tile, :].astype(jnp.float32)
            added = added + grad
            grads[jb % 2, r, t : t + tile, :] = grad.astype(jnp.bfloat16)
        total[jb, t : t + tile, :] = added

    def query_grad(jb, r):
        dq_s[r, jb] = (dot(k_s[r, :c, :], grads[jb % 2, r], ((1,), (0,))) * scaling).astype(jnp.bfloat16)

    def add_to(at, r, jb, part):
        if jb:
            part = part + dkv[r, at : at + c, :]
        dkv[r, at : at + c, :] = part

    def key_grad(jb, r):
        add_to(0, r, jb, dot(q_s[r, jb, :c, :], grads[jb % 2, r], ((1,), (1,))))

    def value_grad(jb, r):
        add_to(c, r, jb, dot(scaled[jb, r], weights[jb % 2, r], ((1,), (1,))))

    def each(step, jb, *ranges):
        if not 0 <= jb < n_col:
            return []
        return [functools.partial(step, jb, *at) for at in itertools.product(*ranges)]

    def finish(jb):
        return each(value_grad, jb, some) + each(query_grad, jb, some) + each(key_grad, jb, some)

    woven(each(score, 0, some, tiles))
    for jb in range(n_col):
        woven(each(expand, jb, some, tiles), finish(jb - 1))
        woven(each(attend, jb, some), each(score, jb + 1, some, tiles[: len(tiles) // 2]))
        woven(each(back, jb, tiles), each(score, jb + 1, some, tiles[len(tiles) // 2 :]))
    woven(finish(n_col - 1))

    for r in some:
        for step in range(n_col):
            jb = peer_of(me, step)
            span = pl.ds(pl.multiple_of(jb * blk, blk), blk)
            outs[step][rows_of(r, 0), :] = dq_s[r, jb]
            outs[step][rows_of(r, 1), :] = (dkv[r, :c, span] * (1.0 / LOG2E)).astype(jnp.bfloat16)
            outs[step][rows_of(r, 2), :] = dkv[r, c:, span].astype(jnp.bfloat16)
            outs[step][rows_of(r, 3), :] = at_s[r, jb]

    if last:

        @pl.when(pl.program_id(0) == pl.num_programs(0) - 1)
        def _():
            mine, others = totals
            pairs, _, width = mine.shape
            for pair in range(pairs):
                at = 2 * pair * width
                both = total[at // blk, :, at % blk : at % blk + 2 * width].astype(jnp.bfloat16)
                even, odd = both[:, :width], both[:, width:]
                place = peer_of(level, pair)
                mine[place] = jnp.where(side == 0, even, odd)
                others[place] = jnp.where(side == 0, odd, even)


def hold_kernel(*refs):
    pass


def params(mib):
    return pltpu.CompilerParams(
        dimension_semantics=("arbitrary",), vmem_limit_bytes=mib * 1024 * 1024
    )


def on_device(n_row, n_col, query, key, value, gate, d_out, bias, length):
    rows, blk, channels = query.shape
    heads, _, n = bias.shape
    c = channels // heads
    groups = n_col // heads
    share = rows // groups
    sizes = [share * weight // sum(SHARES) for weight in SHARES]
    starts = [sizes[-1] + sum(sizes[:m]) for m in range(len(sizes) - 1)] + [0]
    assert groups * heads == n_col and n == n_col * blk and groups * sum(sizes) == rows
    scaling = c ** (-0.5)
    per = 2 if all(size % 2 == 0 for size in sizes) else 1
    split_rows = (groups, share, blk, channels)
    query, key, value, gate, d_out = (x.reshape(split_rows) for x in (query, key, value, gate, d_out))
    row = lax.axis_index("row")
    info = jnp.stack([length[0], lax.axis_index("col"), row % 2, row // 2]).astype(jnp.int32)
    width = n // n_row
    lines = PIECES * c
    chunks = len(sizes)

    untouched = pl.BlockSpec(memory_space=pl.ANY)

    def exchange(blocks):
        pairs = [[(a, a ^ step) for a in range(n_col)] for step in range(n_col)]
        return [blocks[0]] + [lax.ppermute(blocks[step], "col", pairs[step]) for step in range(1, n_col)]

    def swap(x):
        return lax.ppermute(x, "row", [(r, r ^ 1) for r in range(n_row)])

    def hold(blocks, until):
        count = len(blocks)
        return pl.pallas_call(
            hold_kernel,
            in_specs=[untouched] * (count + len(until)),
            out_specs=[untouched] * count,
            out_shape=[jax.ShapeDtypeStruct(x.shape, x.dtype) for x in blocks],
            input_output_aliases={a: a for a in range(count)},
            compiler_params=pltpu.CompilerParams(vmem_limit_bytes=1024 * 1024),
            name="hold",
        )(*blocks, *until)

    def call(kernel, name, flops, grid, operands, out_specs, out_shape, scratch, aliases):
        return pl.pallas_call(
            kernel,
            grid_spec=pltpu.PrefetchScalarGridSpec(
                num_scalar_prefetch=1,
                grid=(grid,),
                in_specs=[spec for spec, _ in operands],
                out_specs=out_specs,
                scratch_shapes=scratch,
            ),
            out_shape=out_shape,
            input_output_aliases=aliases,
            compiler_params=params({"pack": 60, "attend": 26, "unpack": 24}[name]),
            cost_estimate=pl.CostEstimate(flops=flops, bytes_accessed=1, transcendentals=0),
            name=name,
        )(info, *[x for _, x in operands])

    def still(*shape):
        return pl.BlockSpec(shape, lambda i, info: (0,) * len(shape), pipeline_mode=pl.Buffered(1))

    def part(size, skip):
        return pl.BlockSpec((size, blk), lambda i, info: (skip + i, 0))

    def rows_a_step(*counts):
        return max(step for step in range(1, 6) if all(count % step == 0 for count in counts))

    def rows_of(group):
        return starts[group[0]], sum(sizes[m] for m in group)

    def pack(group):
        with_bias = group[0] == 0
        start, count = rows_of(group)
        step = rows_a_step(start, count)
        assert not with_bias or step == count
        base = start // step
        whole = pl.BlockSpec((groups, step, blk, channels), lambda i, info: (0, base + i, 0, 0))
        ahead = [n] + [n // 2] * (n_col - 1) if with_bias else [0] * n_col
        size = count * lines
        operands = [(whole, x) for x in (query, key, value, gate, d_out)]
        if with_bias:
            operands.append((still(heads, blk, n), bias))
        return call(
            functools.partial(pack_kernel, heads, groups, with_bias),
            "pack",
            count * 10**6,
            count // step,
            operands,
            [part(x + step * lines, 0) for x in ahead],
            [jax.ShapeDtypeStruct((x + size, blk), jnp.bfloat16) for x in ahead],
            [pltpu.VMEM((groups, step, PIECES, channels, blk), jnp.bfloat16)],
            {},
        )

    def attend(m, total, bias_blocks, blocks, room):
        first, last = m == 0, m == chunks - 1

        def scratch(*shape, dtype=jnp.bfloat16):
            return pltpu.VMEM((per, *shape), dtype)

        operands = [(still(n if a == 0 else n // 2, blk), x) for a, x in enumerate(bias_blocks)]
        (inward,) = [group for group in INWARD if m in group]
        (outward,) = [group for group in OUTWARD if m in group]
        behind = sum(sizes[o] for o in inward if o < m) // per
        ahead = sum(sizes[o] for o in outward if o < m) // per
        for a, x in enumerate(blocks):
            skip = (n if a == 0 else n // 2) // (per * lines) if first else behind
            operands.append((part(per * lines, skip), x))
        square = (n_col, n, blk)
        aliases = {}
        if not first:
            operands.append((still(*square), total))
        if ahead:
            aliases |= {1 + len(operands) + a: a for a in range(n_col)}
            operands += [(untouched, x) for x in room]
        size = rows_of(outward)[1]
        out_shape = [jax.ShapeDtypeStruct((size * lines, blk), jnp.bfloat16)] * n_col
        if last:
            totals = [jax.ShapeDtypeStruct((n_row // 2, n, width), jnp.bfloat16)] * 2
        else:
            totals = [jax.ShapeDtypeStruct(square, jnp.float32)]
        deep = 4 * c
        result = call(
            functools.partial(attention_kernel, n_col, per, c, scaling, first, last),
            "attend",
            sizes[m] * 4 * 10**9,
            sizes[m] // per,
            operands,
            [part(per * lines, ahead)] * n_col
            + [still(*x.shape) for x in totals]
            + [still(8, 128)],
            out_shape + totals + [jax.ShapeDtypeStruct((8, 128), jnp.float32)],
            [
                pltpu.VMEM(square, jnp.float32),
                pltpu.VMEM(square if last else (8, 128), jnp.float32),
                scratch(n_col, deep, blk),
                scratch(n_col, c, blk),
                scratch(deep, n),
                scratch(deep, n),
                scratch(n, deep),
                scratch(n, deep),
                scratch(n_col, c, blk),
                scratch(n_col, c, blk),
                scratch(2 * c, n, dtype=jnp.float32),
                pltpu.VMEM((2, per, n, blk), jnp.float32),
                pltpu.VMEM((2, per, n, blk), jnp.bfloat16),
                pltpu.VMEM((2, per, n, blk), jnp.bfloat16),
            ],
            aliases,
        )
        return result[:n_col], result[n_col:-1], result[-1]

    def unpack(group, blocks, grads):
        start, count = rows_of(group)
        step = rows_a_step(start, count)
        base = start // step
        whole = pl.BlockSpec((groups, step, blk, channels), lambda i, info: (0, base + i, 0, 0))
        kept = [] if grads is None else list(grads)
        operands = [(whole, gate), (whole, d_out)]
        operands += [(part(step * lines, 0), x) for x in blocks]
        aliases = {1 + len(operands) + a: a for a in range(len(kept))}
        operands += [(untouched, x) for x in kept]
        return call(
            functools.partial(unpack_kernel, heads, groups),
            "unpack",
            1,
            count // step,
            operands,
            [whole] * 4 + [pl.BlockSpec((8, 128), lambda i, info: (0, 0))],
            [jax.ShapeDtypeStruct(query.shape, jnp.bfloat16)] * 4
            + [jax.ShapeDtypeStruct((8, 128), jnp.float32)],
            [pltpu.VMEM((groups, step, PIECES, channels, blk), jnp.bfloat16)],
            aliases,
        )

    packed = [pack(group) for group in INWARD]
    own, *fetched = exchange(packed[0])
    fetched = hold(fetched, [x[0] for x in packed[1:]])
    tables = [own, *fetched] + [swap(x) for x in fetched]
    arrived = {0: [own, *fetched]}

    totals, results, sent, done = [None], None, [], []
    for m in range(chunks):
        at = [m in group for group in INWARD].index(True)
        for ahead in range(at + 1, min(at + 2, len(INWARD) - 1) + 1):
            if ahead not in arrived and (ahead == 1 or m >= INWARD[ahead - 1][0]):
                until = arrived[ahead - 1][1:] + (done[m - 1 : m] if m else [])
                arrived[ahead] = exchange([packed[ahead][0], *hold(packed[ahead][1:], until)])
        results, totals, token = attend(m, totals[0], tables, arrived[at], results)
        done.append(token)
        if m in [group[-1] for group in OUTWARD]:
            sent.append(exchange(results))
    grads, tokens = None, []
    for group, blocks in zip(OUTWARD, sent):
        *grads, token = unpack(group, blocks, grads)
        tokens.append(token)

    mine, others = totals
    (others,) = hold([others], sent[0][1:])
    others = swap(others)
    total = mine[0].astype(jnp.float32) + others[0].astype(jnp.float32)
    for step in range(1, n_row // 2):
        share = mine[step].astype(jnp.float32) + others[step].astype(jnp.float32)
        pairs = [(r, r ^ (2 * step)) for r in range(n_row)]
        total += lax.ppermute(share.astype(jnp.bfloat16), "row", pairs).astype(jnp.float32)
    total = (total + tokens[-2][0, 0]).astype(jnp.bfloat16).reshape(n_col, blk, width)
    total = lax.all_to_all(total, "col", split_axis=0, concat_axis=0, tiled=True)
    total = jnp.sum(total.reshape(heads, groups, blk, width).astype(jnp.float32), axis=1)
    bias_grad = jnp.transpose(total, (0, 2, 1))
    d_query, d_key, d_value, d_gate = (x.reshape(rows, blk, channels) for x in grads)
    return d_query, d_key, d_value, d_gate, bias_grad


def solution(mesh):
    pair = P("row", "col", None)
    return jax.shard_map(
        functools.partial(on_device, mesh.shape["row"], mesh.shape["col"]),
        mesh=mesh,
        in_specs=(pair, pair, pair, pair, pair, P(None, "col", None), P()),
        out_specs=(pair, pair, pair, pair, P(None, "row", "col")),
        check_vma=False,
    )
```

profile of v0, /device:TPU:18, one launch (start us, length us, event | category | flops | bytes accessed | tf_op | source)
XLA Modules:
  0.0 191.4 jit_solution(10246819371509457156)
XLA Ops:
  1.9 4.1 %pack.4 = (bf16[1280,256]{1,0:T(8,128)(2,1)}, bf16[768,256]{1,0:T(8,128)(2,1)}, bf16[768,256]{1,0:T(8,128)(2,1)}, bf16[768,256]{1,0:T(8,128)(2,1)}) custom-call(s32[4]{0:T(128)} %pad_add_fusion.info, bf16[1,24,256,128]{3,2,1,0:T(8,128)(2,1)} %bitcast.44, bf16[1,24,256,128]{3,2,1,0:T(8,128)(2,1)} %bitcast.48, bf16[1,24,256,128]{3,2,1,0:T(8,128)(2,1)} %bitcast.52, ...), custom_call_target="tpu_custom_call" | custom-call | flops 2000000 | bytes 1 | tf_op jit(solution)/shard_map/pack/pallas_call | solution.py:281
  6.6 1.5 collective-permute-start.1
  8.1 1.4 collective-permute-start.2
  9.5 3.2 %pack.5 = (bf16[512,256]{1,0:T(8,128)(2,1)}, bf16[512,256]{1,0:T(8,128)(2,1)}, bf16[512,256]{1,0:T(8,128)(2,1)}, bf16[512,256]{1,0:T(8,128)(2,1)}) custom-call(s32[4]{0:T(128)} %pad_add_fusion.info, bf16[1,24,256,128]{3,2,1,0:T(8,128)(2,1)} %bitcast.45, bf16[1,24,256,128]{3,2,1,0:T(8,128)(2,1)} %bitcast.49, bf16[1,24,256,128]{3,2,1,0:T(8,128)(2,1)} %bitcast.53, ...), custom_call_target="tpu_custom_call" | custom-call | flops 4000000 | bytes 1 | tf_op jit(solution)/shard_map/pack/pallas_call | solution.py:281
  12.8 3.7 %pack.6 = (bf16[1024,256]{1,0:T(8,128)(2,1)}, bf16[1024,256]{1,0:T(8,128)(2,1)}, bf16[1024,256]{1,0:T(8,128)(2,1)}, bf16[1024,256]{1,0:T(8,128)(2,1)}) custom-call(s32[4]{0:T(128)} %pad_add_fusion.info, bf16[1,24,256,128]{3,2,1,0:T(8,128)(2,1)} %bitcast.46, bf16[1,24,256,128]{3,2,1,0:T(8,128)(2,1)} %bitcast.50, bf16[1,24,256,128]{3,2,1,0:T(8,128)(2,1)} %bitcast.54, ...), custom_call_target="tpu_custom_call" | custom-call | flops 8000000 | bytes 1 | tf_op jit(solution)/shard_map/pack/pallas_call | solution.py:281
  16.5 4.2 %pack.7 = (bf16[1280,256]{1,0:T(8,128)(2,1)}, bf16[1280,256]{1,0:T(8,128)(2,1)}, bf16[1280,256]{1,0:T(8,128)(2,1)}, bf16[1280,256]{1,0:T(8,128)(2,1)}) custom-call(s32[4]{0:T(128)} %pad_add_fusion.info, bf16[1,24,256,128]{3,2,1,0:T(8,128)(2,1)} %bitcast.47, bf16[1,24,256,128]{3,2,1,0:T(8,128)(2,1)} %bitcast.51, bf16[1,24,256,128]{3,2,1,0:T(8,128)(2,1)} %bitcast.55, ...), custom_call_target="tpu_custom_call" | custom-call | flops 10000000 | bytes 1 | tf_op jit(solution)/shard_map/pack/pallas_call | solution.py:281
  20.6 4.3 %collective-permute-done.1.refs_1_ = bf16[768,256]{1,0:T(8,128)(2,1)S(1)} collective-permute-done((bf16[768,256]{1,0:T(8,128)(2,1)}, bf16[768,256]{1,0:T(8,128)(2,1)S(1)}, u32[]{:S(2)}, u32[]{:S(2)}) %collective-permute-start.1) | collective-permute-done | bytes 393248 | tf_op jit(solution)/shard_map/ppermute | solution.py:263
  25.0 1.5 collective-permute-done.2.refs_2_
  26.5 1.1 copy-done.4
  29.0 1.5 collective-permute-start.7
  30.6 1.2 collective-permute-start.8
  31.8 7.9 %attend.4 = (bf16[1792,256]{1,0:T(8,128)(2,1)S(1)}, bf16[1792,256]{1,0:T(8,128)(2,1)S(1)}, bf16[1792,256]{1,0:T(8,128)(2,1)S(1)}, bf16[1792,256]{1,0:T(8,128)(2,...) custom-call(s32[4]{0:T(128)S(1)} %copy-done.17, bf16[1280,256]{1,0:T(8,128)(2,1)S(1)} %copy-done.18, ...), custom_call_target="tpu_custom_call" | custom-call | flops 8000000000 | bytes 1 | tf_op jit(solution)/shard_map/attend/pallas_call | solution.py:281
  39.7 3.4 %collective-permute-done.7.refs_4_.refs_9_ = bf16[512,256]{1,0:T(8,128)(2,1)S(1)} collective-permute-done((bf16[512,256]{1,0:T(8,128)(2,1)S(1)}, bf16[512,256]{1,0:T(8,128)(2,1)S(1)}, u32[]{:S(2)}, u32[]{:S(2)}) %collective-permute-start.7) | collective-permute-done | bytes 262176 | tf_op jit(solution)/shard_map/ppermute | solution.py:263
  43.1 1.3 collective-permute-start.9
  45.2 1.4 collective-permute-start.11
  46.6 15.7 %attend.5 = (bf16[1792,256]{1,0:T(8,128)(2,1)S(1)}, bf16[1792,256]{1,0:T(8,128)(2,1)S(1)}, bf16[1792,256]{1,0:T(8,128)(2,1)S(1)}, bf16[1792,256]{1,0:T(8,128)(2,...) custom-call(s32[4]{0:T(128)S(1)} %copy-done.17, ...), custom_call_target="tpu_custom_call", output_to_operand_aliasing={{0}: (13, {}), {1}: (14, {}), {2}: (15, {}), {3}: (16, {})} | custom-call | flops 16000000000 | bytes 1 | tf_op jit(solution)/shard_map/attend/pallas_call | solution.py:281
  62.3 6.5 %collective-permute-done.10.refs_4_.refs_9_ = bf16[1024,256]{1,0:T(8,128)(2,1)S(1)} collective-permute-done((bf16[1024,256]{1,0:T(8,128)(2,1)S(1)}, bf16[1024,256]{1,0:T(8,128)(2,1)S(1)}, u32[]{:S(2)}, u32[]{:S(2)}) %collective-permute-start.10) | collective-permute-done | bytes 524320 | tf_op jit(solution)/shard_map/ppermute | solution.py:263
  69.5 1.2 collective-permute-start.13
  70.7 1.7 collective-permute-start.14
  72.4 30.0 %attend.6 = (bf16[1792,256]{1,0:T(8,128)(2,1)S(1)}, bf16[1792,256]{1,0:T(8,128)(2,1)S(1)}, bf16[1792,256]{1,0:T(8,128)(2,1)S(1)}, bf16[1792,256]{1,0:T(8,128)(2,...) custom-call(s32[4]{0:T(128)S(1)} %copy-done.17, ...), custom_call_target="tpu_custom_call", output_to_operand_aliasing={{0}: (13, {}), {1}: (14, {}), {2}: (15, {}), {3}: (16, {})} | custom-call | flops 32000000000 | bytes 1 | tf_op jit(solution)/shard_map/attend/pallas_call | solution.py:281
  103.0 1.2 collective-permute-start.19
  104.2 1.7 collective-permute-start.20
  106.0 37.5 %attend.7 = (bf16[1280,256]{1,0:T(8,128)(2,1)S(1)}, bf16[1280,256]{1,0:T(8,128)(2,1)}, bf16[1280,256]{1,0:T(8,128)(2,1)}, bf16[1280,256]{1,0:T(8,128)(2,1)}, bf1...) custom-call(s32[4]{0:T(128)S(1)} %copy-done.17, ...), custom_call_target="tpu_custom_call" | custom-call | flops 40000000000 | bytes 1 | tf_op jit(solution)/shard_map/attend/pallas_call | solution.py:281
  144.3 2.7 %collective-permute-done.21 = bf16[4,1024,128]{2,1,0:T(8,128)(2,1)S(1)} collective-permute-done((bf16[4,1024,128]{2,1,0:T(8,128)(2,1)S(1)}, bf16[4,1024,128]{2,1,0:T(8,128)(2,1)S(1)}, u32[]{:S(2)}, u32[]{:S(2)}) %collective-permute-start.21) | collective-permute-done | bytes 1048608 | tf_op jit(solution)/shard_map/ppermute | solution.py:266
  147.7 3.5 %collective-permute-start.23 = (bf16[1024,128]{1,0:T(8,128)(2,1)S(1)}, bf16[1024,128]{1,0:T(8,128)(2,1)S(1)}, u32[]{:S(2)}, u32[]{:S(2)}) collective-permute-start(bf16[1024,128]{1,0:T(8,128)(2,1)S(1)} %get-tuple-element.127), channel_id=1, source_target_pairs={{0,16},{4,20},{8,24},{12,28},{16,0},{20,4},{24,8},{28,12},{1,17},{... | collective-permute-start | bytes 786440 | tf_op jit(solution)/shard_map/ppermute | solution.py:443
  151.8 1.2 collective-permute-start.16
  153.0 14.7 %collective-permute-done.24 = bf16[1024,128]{1,0:T(8,128)(2,1)S(1)} collective-permute-done((bf16[1024,128]{1,0:T(8,128)(2,1)S(1)}, bf16[1024,128]{1,0:T(8,128)(2,1)S(1)}, u32[]{:S(2)}, u32[]{:S(2)}) %collective-permute-start.24) | collective-permute-done | bytes 262176 | tf_op jit(solution)/shard_map/ppermute | solution.py:443
  167.7 1.2 collective-permute-start.17
  168.9 4.4 %unpack.2 = (bf16[1,24,256,128]{3,2,1,0:T(8,128)(2,1)}, bf16[1,24,256,128]{3,2,1,0:T(8,128)(2,1)}, bf16[1,24,256,128]{3,2,1,0:T(8,128)(2,1)}, bf16[1,24,256,128]{3,2,1,0:T(8,128)(2,1)}, f32[8,128]{1,0:T(8,128)S(1)}) custom-call(s32[4]{0:T(128)S(1)} %copy-done.17, bf16[1,24,256,128]{3,2,1,0:T(8,128)(2,1)S(1)} %bitcast.36, ...), custom_call_target="tpu_custom_call" | custom-call | flops 1 | bytes 1 | tf_op jit(solution)/shard_map/unpack/pallas_call | solution.py:281
  175.5 4.2 %all-to-all-start = ((bf16[4,256,128]{1,2,0:T(8,128)(2,1)}), bf16[4,256,128]{1,2,0:T(8,128)(2,1)S(1)}, u32[]{:S(2)}, u32[]{:S(2)}) async-start(bf16[4,256,128]{1,2,0:T(8,128)(2,1)} %copy.37), calls=%async_computation | async-start | bytes 524288 | tf_op jit(solution)/shard_map/all_to_all | solution.py:445
  179.7 5.9 %collective-permute-done.17.refs_3_ = bf16[1280,256]{1,0:T(8,128)(2,1)} collective-permute-done((bf16[1280,256]{1,0:T(8,128)(2,1)}, bf16[1280,256]{1,0:T(8,128)(2,1)}, u32[]{:S(2)}, u32[]{:S(2)}) %collective-permute-start.17) | collective-permute-done | bytes 655392 | tf_op jit(solution)/shard_map/ppermute | solution.py:263
  186.7 3.8 %unpack.3 = (bf16[1,24,256,128]{3,2,1,0:T(8,128)(2,1)}, bf16[1,24,256,128]{3,2,1,0:T(8,128)(2,1)}, bf16[1,24,256,128]{3,2,1,0:T(8,128)(2,1)}, bf16[1,24,256,128]{3,2,1,0:T(8,128)(2,1)}, f32[8,128]{1,0:T(8,128)}) custom-call(s32[4]{0:T(128)S(1)} %copy-done.17, ...), custom_call_target="tpu_custom_call", output_to_operand_aliasing={{0}: (7, {}), {1}: (8, {}), {2}: (9, {}), {3}: (10, {})} | custom-call | flops 1 | bytes 1 | tf_op jit(solution)/shard_map/unpack/pallas_call | solution.py:281
  (79 shorter events, 11.1 us)
Async XLA Ops:
  6.0 14.6 %collective-permute-start = (bf16[768,256]{1,0:T(8,128)(2,1)}, bf16[768,256]{1,0:T(8,128)(2,1)S(1)}, u32[]{:S(2)}, u32[]{:S(2)}) collective-permute-start(bf16[768,256]{1,0:T(8,128)(2,1)} %get-tuple-element.66), channel_id=1, source_target_pairs={{0,1},{1,0},{2,3},{3,2},{4,5},{5,4},{6,7},{7,6},{8,9},{9,8},{10,11... | collective-permute-start | bytes 1179656 | tf_op jit(solution)/shard_map/ppermute | solution.py:263
  6.6 18.4 %collective-permute-start.1 = (bf16[768,256]{1,0:T(8,128)(2,1)}, bf16[768,256]{1,0:T(8,128)(2,1)S(1)}, u32[]{:S(2)}, u32[]{:S(2)}) collective-permute-start(bf16[768,256]{1,0:T(8,128)(2,1)} %get-tuple-element.67), channel_id=1, source_target_pairs={{0,2},{1,3},{2,0},{3,1},{4,6},{5,7},{6,4},{7,5},{8,10},{9,11},{10,... | collective-permute-start | bytes 1179656 | tf_op jit(solution)/shard_map/ppermute | solution.py:263
  8.1 18.4 %collective-permute-start.2 = (bf16[768,256]{1,0:T(8,128)(2,1)}, bf16[768,256]{1,0:T(8,128)(2,1)S(1)}, u32[]{:S(2)}, u32[]{:S(2)}) collective-permute-start(bf16[768,256]{1,0:T(8,128)(2,1)} %get-tuple-element.68), channel_id=1, source_target_pairs={{0,3},{1,2},{2,1},{3,0},{4,7},{5,6},{6,5},{7,4},{8,11},{9,10},{10,... | collective-permute-start | bytes 1179656 | tf_op jit(solution)/shard_map/ppermute | solution.py:263
  27.6 3.0 %collective-permute-start.3 = (bf16[768,256]{1,0:T(8,128)(2,1)S(1)}, bf16[768,256]{1,0:T(8,128)(2,1)S(1)}, u32[]{:S(2)}, u32[]{:S(2)}) collective-permute-start(bf16[768,256]{1,0:T(8,128)(2,1)S(1)} %get-tuple-element.72.refs_3_.refs_1_.refs_8_), channel_id=1, source_target_pairs={{0,4},{4,0},{8,12},{12,8},{16,20},{20,16},{24,28},{28,24},{1,5},{5... | collective-permute-start | bytes 1179656 | tf_op jit(solution)/shard_map/ppermute | solution.py:266
  27.6 4.2 %collective-permute-start.4 = (bf16[768,256]{1,0:T(8,128)(2,1)S(1)}, bf16[768,256]{1,0:T(8,128)(2,1)S(1)}, u32[]{:S(2)}, u32[]{:S(2)}) collective-permute-start(bf16[768,256]{1,0:T(8,128)(2,1)S(1)} %get-tuple-element.73.refs_4_.refs_2_.refs_9_), channel_id=1, source_target_pairs={{0,4},{4,0},{8,12},{12,8},{16,20},{20,16},{24,28},{28,24},{1,5},{5... | collective-permute-start | bytes 1179656 | tf_op jit(solution)/shard_map/ppermute | solution.py:266
  28.1 3.7 %collective-permute-start.5 = (bf16[768,256]{1,0:T(8,128)(2,1)S(1)}, bf16[768,256]{1,0:T(8,128)(2,1)S(1)}, u32[]{:S(2)}, u32[]{:S(2)}) collective-permute-start(bf16[768,256]{1,0:T(8,128)(2,1)S(1)} %get-tuple-element.74.refs_5_.refs_3_.refs_10_), channel_id=1, source_target_pairs={{0,4},{4,0},{8,12},{12,8},{16,20},{20,16},{24,28},{28,24},{1,5},{5... | collective-permute-start | bytes 1179656 | tf_op jit(solution)/shard_map/ppermute | solution.py:266
  28.2 11.5 %collective-permute-start.6 = (bf16[512,256]{1,0:T(8,128)(2,1)S(1)}, bf16[512,256]{1,0:T(8,128)(2,1)S(1)}, u32[]{:S(2)}, u32[]{:S(2)}) collective-permute-start(bf16[512,256]{1,0:T(8,128)(2,1)S(1)} %get-tuple-element.84), channel_id=1, source_target_pairs={{0,1},{1,0},{2,3},{3,2},{4,5},{5,4},{6,7},{7,6},{8,9},{9,8},{10,11... | collective-permute-start | bytes 786440 | tf_op jit(solution)/shard_map/ppermute | solution.py:263
  29.0 14.0 %collective-permute-start.7 = (bf16[512,256]{1,0:T(8,128)(2,1)S(1)}, bf16[512,256]{1,0:T(8,128)(2,1)S(1)}, u32[]{:S(2)}, u32[]{:S(2)}) collective-permute-start(bf16[512,256]{1,0:T(8,128)(2,1)S(1)} %get-tuple-element.85), channel_id=1, source_target_pairs={{0,2},{1,3},{2,0},{3,1},{4,6},{5,7},{6,4},{7,5},{8,10},{9,11},{10,... | collective-permute-start | bytes 786440 | tf_op jit(solution)/shard_map/ppermute | solution.py:263
  30.6 12.5 %collective-permute-start.8 = (bf16[512,256]{1,0:T(8,128)(2,1)S(1)}, bf16[512,256]{1,0:T(8,128)(2,1)S(1)}, u32[]{:S(2)}, u32[]{:S(2)}) collective-permute-start(bf16[512,256]{1,0:T(8,128)(2,1)S(1)} %get-tuple-element.86), channel_id=1, source_target_pairs={{0,3},{1,2},{2,1},{3,0},{4,7},{5,6},{6,5},{7,4},{8,11},{9,10},{10,... | collective-permute-start | bytes 786440 | tf_op jit(solution)/shard_map/ppermute | solution.py:263
  43.1 19.3 %collective-permute-start.9 = (bf16[1024,256]{1,0:T(8,128)(2,1)S(1)}, bf16[1024,256]{1,0:T(8,128)(2,1)S(1)}, u32[]{:S(2)}, u32[]{:S(2)}) collective-permute-start(bf16[1024,256]{1,0:T(8,128)(2,1)S(1)} %get-tuple-element.88), channel_id=1, source_target_pairs={{0,1},{1,0},{2,3},{3,2},{4,5},{5,4},{6,7},{7,6},{8,9},{9,8},{10,11... | collective-permute-start | bytes 1572872 | tf_op jit(solution)/shard_map/ppermute | solution.py:263
  44.4 24.4 %collective-permute-start.10 = (bf16[1024,256]{1,0:T(8,128)(2,1)S(1)}, bf16[1024,256]{1,0:T(8,128)(2,1)S(1)}, u32[]{:S(2)}, u32[]{:S(2)}) collective-permute-start(bf16[1024,256]{1,0:T(8,128)(2,1)S(1)} %get-tuple-element.89), channel_id=1, source_target_pairs={{0,2},{1,3},{2,0},{3,1},{4,6},{5,7},{6,4},{7,5},{8,10},{9,11},{10,... | collective-permute-start | bytes 1572872 | tf_op jit(solution)/shard_map/ppermute | solution.py:263
  45.2 23.6 %collective-permute-start.11 = (bf16[1024,256]{1,0:T(8,128)(2,1)S(1)}, bf16[1024,256]{1,0:T(8,128)(2,1)S(1)}, u32[]{:S(2)}, u32[]{:S(2)}) collective-permute-start(bf16[1024,256]{1,0:T(8,128)(2,1)S(1)} %get-tuple-element.90), channel_id=1, source_target_pairs={{0,3},{1,2},{2,1},{3,0},{4,7},{5,6},{6,5},{7,4},{8,11},{9,10},{10,... | collective-permute-start | bytes 1572872 | tf_op jit(solution)/shard_map/ppermute | solution.py:263
  46.6 22.2 %copy-start.6 = (bf16[1280,256]{1,0:T(8,128)(2,1)S(1)}, bf16[1280,256]{1,0:T(8,128)(2,1)}, u32[]{:S(2)}) copy-start(bf16[1280,256]{1,0:T(8,128)(2,1)} %get-tuple-element.75.refs_0_) | copy-start | bytes 1966084
  46.6 22.2 %copy-start.7 = (bf16[1280,256]{1,0:T(8,128)(2,1)S(1)}, bf16[1280,256]{1,0:T(8,128)(2,1)}, u32[]{:S(2)}) copy-start(bf16[1280,256]{1,0:T(8,128)(2,1)} %get-tuple-element.76.refs_1_) | copy-start | bytes 1966084
  46.6 22.2 %copy-start.8 = (bf16[1280,256]{1,0:T(8,128)(2,1)S(1)}, bf16[1280,256]{1,0:T(8,128)(2,1)}, u32[]{:S(2)}) copy-start(bf16[1280,256]{1,0:T(8,128)(2,1)} %get-tuple-element.77.refs_2_) | copy-start | bytes 1966084
  68.8 35.4 %collective-permute-start.12 = (bf16[1280,256]{1,0:T(8,128)(2,1)S(1)}, bf16[1280,256]{1,0:T(8,128)(2,1)S(1)}, u32[]{:S(2)}, u32[]{:S(2)}) collective-permute-start(bf16[1280,256]{1,0:T(8,128)(2,1)S(1)} %get-tuple-element.97), channel_id=1, source_target_pairs={{0,1},{1,0},{2,3},{3,2},{4,5},{5,4},{6,7},{7,6},{8,9},{9,8},{10,11... | collective-permute-start | bytes 1966088 | tf_op jit(solution)/shard_map/ppermute | solution.py:263
  69.5 36.5 %collective-permute-start.13 = (bf16[1280,256]{1,0:T(8,128)(2,1)S(1)}, bf16[1280,256]{1,0:T(8,128)(2,1)S(1)}, u32[]{:S(2)}, u32[]{:S(2)}) collective-permute-start(bf16[1280,256]{1,0:T(8,128)(2,1)S(1)} %get-tuple-element.98), channel_id=1, source_target_pairs={{0,2},{1,3},{2,0},{3,1},{4,6},{5,7},{6,4},{7,5},{8,10},{9,11},{10,... | collective-permute-start | bytes 1966088 | tf_op jit(solution)/shard_map/ppermute | solution.py:263
  70.7 35.3 %collective-permute-start.14 = (bf16[1280,256]{1,0:T(8,128)(2,1)S(1)}, bf16[1280,256]{1,0:T(8,128)(2,1)S(1)}, u32[]{:S(2)}, u32[]{:S(2)}) collective-permute-start(bf16[1280,256]{1,0:T(8,128)(2,1)S(1)} %get-tuple-element.99), channel_id=1, source_target_pairs={{0,3},{1,2},{2,1},{3,0},{4,7},{5,6},{6,5},{7,4},{8,11},{9,10},{10,... | collective-permute-start | bytes 1966088 | tf_op jit(solution)/shard_map/ppermute | solution.py:263
  72.4 33.6 %copy-start.5 = (bf16[1280,256]{1,0:T(8,128)(2,1)S(1)}, bf16[1280,256]{1,0:T(8,128)(2,1)}, u32[]{:S(2)}) copy-start(bf16[1280,256]{1,0:T(8,128)(2,1)} %get-tuple-element.71.refs_5_.refs_7_) | copy-start | bytes 1966084
  102.4 41.1 %collective-permute-start.18 = (bf16[1792,256]{1,0:T(8,128)(2,1)S(1)}, bf16[1792,256]{1,0:T(8,128)(2,1)S(1)}, u32[]{:S(2)}, u32[]{:S(2)}) collective-permute-start(bf16[1792,256]{1,0:T(8,128)(2,1)S(1)} %get-tuple-element.111), channel_id=1, source_target_pairs={{0,1},{1,0},{2,3},{3,2},{4,5},{5,4},{6,7},{7,6},{8,9},{9,8},{10,11... | collective-permute-start | bytes 2752520 | tf_op jit(solution)/shard_map/ppermute | solution.py:263
  103.0 40.5 %collective-permute-start.19 = (bf16[1792,256]{1,0:T(8,128)(2,1)S(1)}, bf16[1792,256]{1,0:T(8,128)(2,1)S(1)}, u32[]{:S(2)}, u32[]{:S(2)}) collective-permute-start(bf16[1792,256]{1,0:T(8,128)(2,1)S(1)} %get-tuple-element.112), channel_id=1, source_target_pairs={{0,2},{1,3},{2,0},{3,1},{4,6},{5,7},{6,4},{7,5},{8,10},{9,11},{10,... | collective-permute-start | bytes 2752520 | tf_op jit(solution)/shard_map/ppermute | solution.py:263
  104.2 39.3 %collective-permute-start.20 = (bf16[1792,256]{1,0:T(8,128)(2,1)S(1)}, bf16[1792,256]{1,0:T(8,128)(2,1)S(1)}, u32[]{:S(2)}, u32[]{:S(2)}) collective-permute-start(bf16[1792,256]{1,0:T(8,128)(2,1)S(1)} %get-tuple-element.113), channel_id=1, source_target_pairs={{0,3},{1,2},{2,1},{3,0},{4,7},{5,6},{6,5},{7,4},{8,11},{9,10},{10,... | collective-permute-start | bytes 2752520 | tf_op jit(solution)/shard_map/ppermute | solution.py:263
  143.5 25.4 %copy-start.1 = (bf16[24,256,128]{2,1,0:T(8,128)(2,1)S(1)}, bf16[24,256,128]{2,1,0:T(8,128)(2,1)}, u32[]{:S(2)}) copy-start(bf16[24,256,128]{2,1,0:T(8,128)(2,1)} %param.11) | copy-start | bytes 4718596
  144.3 24.6 %copy-start = (bf16[24,256,128]{2,1,0:T(8,128)(2,1)S(1)}, bf16[24,256,128]{2,1,0:T(8,128)(2,1)}, u32[]{:S(2)}) copy-start(bf16[24,256,128]{2,1,0:T(8,128)(2,1)} %param.10) | copy-start | bytes 4718596
  144.3 2.7 %collective-permute-start.21 = (bf16[4,1024,128]{2,1,0:T(8,128)(2,1)S(1)}, bf16[4,1024,128]{2,1,0:T(8,128)(2,1)S(1)}, u32[]{:S(2)}, u32[]{:S(2)}) collective-permute-start(bf16[4,1024,128]{2,1,0:T(8,128)(2,1)S(1)} %hold.9), channel_id=1, source_target_pairs={{0,4},{4,0},{8,12},{12,8},{16,20},{20,16},{24,28},{28,24},{1,5},{5... | collective-permute-start | bytes 3145736 | tf_op jit(solution)/shard_map/ppermute | solution.py:266
  147.2 20.4 %collective-permute-start.24 = (bf16[1024,128]{1,0:T(8,128)(2,1)S(1)}, bf16[1024,128]{1,0:T(8,128)(2,1)S(1)}, u32[]{:S(2)}, u32[]{:S(2)}) collective-permute-start(bf16[1024,128]{1,0:T(8,128)(2,1)S(1)} %get-tuple-element.126), channel_id=1, source_target_pairs={{0,24},{4,28},{8,16},{12,20},{16,8},{20,12},{24,0},{28,4},{1,25},{... | collective-permute-start | bytes 786440 | tf_op jit(solution)/shard_map/ppermute | solution.py:443
  147.7 26.0 %collective-permute-start.23 = (bf16[1024,128]{1,0:T(8,128)(2,1)S(1)}, bf16[1024,128]{1,0:T(8,128)(2,1)S(1)}, u32[]{:S(2)}, u32[]{:S(2)}) collective-permute-start(bf16[1024,128]{1,0:T(8,128)(2,1)S(1)} %get-tuple-element.127), channel_id=1, source_target_pairs={{0,16},{4,20},{8,24},{12,28},{16,0},{20,4},{24,8},{28,12},{1,17},{... | collective-permute-start | bytes 786440 | tf_op jit(solution)/shard_map/ppermute | solution.py:443
  151.2 22.6 %collective-permute-start.22 = (bf16[1024,128]{1,0:T(8,128)(2,1)S(1)}, bf16[1024,128]{1,0:T(8,128)(2,1)S(1)}, u32[]{:S(2)}, u32[]{:S(2)}) collective-permute-start(bf16[1024,128]{1,0:T(8,128)(2,1)S(1)} %get-tuple-element.125), channel_id=1, source_target_pairs={{0,8},{4,12},{8,0},{12,4},{16,24},{20,28},{24,16},{28,20},{1,9},{5... | collective-permute-start | bytes 786440 | tf_op jit(solution)/shard_map/ppermute | solution.py:443
  151.2 28.5 %collective-permute-start.15 = (bf16[1280,256]{1,0:T(8,128)(2,1)}, bf16[1280,256]{1,0:T(8,128)(2,1)}, u32[]{:S(2)}, u32[]{:S(2)}) collective-permute-start(bf16[1280,256]{1,0:T(8,128)(2,1)} %get-tuple-element.107), channel_id=1, source_target_pairs={{0,1},{1,0},{2,3},{3,2},{4,5},{5,4},{6,7},{7,6},{8,9},{9,8},{10,11... | collective-permute-start | bytes 1966088 | tf_op jit(solution)/shard_map/ppermute | solution.py:263
  151.8 27.9 %collective-permute-start.16 = (bf16[1280,256]{1,0:T(8,128)(2,1)}, bf16[1280,256]{1,0:T(8,128)(2,1)}, u32[]{:S(2)}, u32[]{:S(2)}) collective-permute-start(bf16[1280,256]{1,0:T(8,128)(2,1)} %get-tuple-element.108), channel_id=1, source_target_pairs={{0,2},{1,3},{2,0},{3,1},{4,6},{5,7},{6,4},{7,5},{8,10},{9,11},{10,... | collective-permute-start | bytes 1966088 | tf_op jit(solution)/shard_map/ppermute | solution.py:263
  167.7 17.9 %collective-permute-start.17 = (bf16[1280,256]{1,0:T(8,128)(2,1)}, bf16[1280,256]{1,0:T(8,128)(2,1)}, u32[]{:S(2)}, u32[]{:S(2)}) collective-permute-start(bf16[1280,256]{1,0:T(8,128)(2,1)} %get-tuple-element.109), channel_id=1, source_target_pairs={{0,3},{1,2},{2,1},{3,0},{4,7},{5,6},{6,5},{7,4},{8,11},{9,10},{10,... | collective-permute-start | bytes 1966088 | tf_op jit(solution)/shard_map/ppermute | solution.py:263
  175.5 15.0 %all-to-all-start = ((bf16[4,256,128]{1,2,0:T(8,128)(2,1)}), bf16[4,256,128]{1,2,0:T(8,128)(2,1)S(1)}, u32[]{:S(2)}, u32[]{:S(2)}) async-start(bf16[4,256,128]{1,2,0:T(8,128)(2,1)} %copy.37), calls=%async_computation | async-start | bytes 524288 | tf_op jit(solution)/shard_map/all_to_all | solution.py:445
  (13 other events, 100.5 us)
where the time goes:
time: 193 us; the launch traced here: 191 us
  Pallas kernels  114 us (59%)
  waiting for transfers between devices  38.9 us (20%)
  starting transfers between devices  29.5 us (15%)
  local copies, waits for them, and re-layouts  4.4 us (2%)
  other arithmetic  2.49 us (1%)
    pallas_call x10, Pallas kernels, call(): pl.pallas_call(kernel, grid_spec=pltpu.PrefetchScalarGridSpec(num_scalar_...  114 us
    ppermute x18, waiting for transfers between devices, exchange(): lax.ppermute(blocks[step], 'col', pairs[step])  21.6 us
    ppermute x18, starting transfers between devices, exchange(): lax.ppermute(blocks[step], 'col', pairs[step])  20.7 us
    ppermute x3, waiting for transfers between devices, on_device(): lax.ppermute(share.astype(jnp.bfloat16), 'row', pairs).astype(jnp.float32)  14.7 us
    all_to_all x1, starting transfers between devices, on_device(): lax.all_to_all(total, 'col', split_axis=0, concat_axis=0, tiled=True)  4.19 us
    ppermute x3, starting transfers between devices, on_device(): lax.ppermute(share.astype(jnp.bfloat16), 'row', pairs).astype(jnp.float32)  4.01 us
  transfers between devices with their start and end apart: 26, of which 7 were waited for; matrix products, arithmetic and copies ran while one was open for 1% of the time, Pallas kernels for 58%

commit v1 on v0

--- a/solution.py
+++ b/solution.py
@@ -92,7 +92,7 @@
     length, me, side, level = info[0], info[1], info[2], info[3]
     blk = ins[0].shape[1]
     n = n_col * blk
-    tile = min(256, n)
+    tile = min(512, n)
     tiles = range(0, n, tile)
     deep = k_s.shape[1]
     some = range(together)

time: 193 us -> 192 us (level)
  transfers between devices with their start and end apart: 26 -> 26, of which waited for: 7 -> 7; matrix products, arithmetic and copies ran while one was open for 1% -> 1% of each run, Pallas kernels for 58% -> 57%
where the time goes in v1:
time: 192 us; the launch traced here: 191 us
  Pallas kernels  113 us (59%)
  waiting for transfers between devices  39.2 us (20%)
  starting transfers between devices  29.4 us (15%)
  local copies, waits for them, and re-layouts  4.4 us (2%)
  other arithmetic  2.49 us (1%)
    pallas_call x10, Pallas kernels, call(): pl.pallas_call(kernel, grid_spec=pltpu.PrefetchScalarGridSpec(num_scalar_...  113 us
    ppermute x18, waiting for transfers between devices, exchange(): lax.ppermute(blocks[step], 'col', pairs[step])  21.9 us
    ppermute x18, starting transfers between devices, exchange(): lax.ppermute(blocks[step], 'col', pairs[step])  20.7 us
    ppermute x3, waiting for transfers between devices, on_device(): lax.ppermute(share.astype(jnp.bfloat16), 'row', pairs).astype(jnp.float32)  14.7 us
    all_to_all x1, starting transfers between devices, on_device(): lax.all_to_all(total, 'col', split_axis=0, concat_axis=0, tiled=True)  4.18 us
    ppermute x3, starting transfers between devices, on_device(): lax.ppermute(share.astype(jnp.bfloat16), 'row', pairs).astype(jnp.float32)  4.01 us
  transfers between devices with their start and end apart: 26, of which 7 were waited for; matrix products, arithmetic and copies ran while one was open for 1% of the time, Pallas kernels for 57%

profile of v1, /device:TPU:18, one launch (start us, length us, event | category | flops | bytes accessed | tf_op | source)
XLA Modules:
  0.0 190.5 jit_solution(11161882376106107909)
XLA Ops:
  1.9 4.1 %pack.4 = (bf16[1280,256]{1,0:T(8,128)(2,1)}, bf16[768,256]{1,0:T(8,128)(2,1)}, bf16[768,256]{1,0:T(8,128)(2,1)}, bf16[768,256]{1,0:T(8,128)(2,1)}) custom-call(s32[4]{0:T(128)} %pad_add_fusion.info, bf16[1,24,256,128]{3,2,1,0:T(8,128)(2,1)} %bitcast.44, bf16[1,24,256,128]{3,2,1,0:T(8,128)(2,1)} %bitcast.48, bf16[1,24,256,128]{3,2,1,0:T(8,128)(2,1)} %bitcast.52, ...), custom_call_target="tpu_custom_call" | custom-call | flops 2000000 | bytes 1 | tf_op jit(solution)/shard_map/pack/pallas_call | solution.py:281
  6.6 1.5 collective-permute-start.1
  8.1 1.4 collective-permute-start.2
  9.5 3.2 %pack.5 = (bf16[512,256]{1,0:T(8,128)(2,1)}, bf16[512,256]{1,0:T(8,128)(2,1)}, bf16[512,256]{1,0:T(8,128)(2,1)}, bf16[512,256]{1,0:T(8,128)(2,1)}) custom-call(s32[4]{0:T(128)} %pad_add_fusion.info, bf16[1,24,256,128]{3,2,1,0:T(8,128)(2,1)} %bitcast.45, bf16[1,24,256,128]{3,2,1,0:T(8,128)(2,1)} %bitcast.49, bf16[1,24,256,128]{3,2,1,0:T(8,128)(2,1)} %bitcast.53, ...), custom_call_target="tpu_custom_call" | custom-call | flops 4000000 | bytes 1 | tf_op jit(solution)/shard_map/pack/pallas_call | solution.py:281
  12.8 3.7 %pack.6 = (bf16[1024,256]{1,0:T(8,128)(2,1)}, bf16[1024,256]{1,0:T(8,128)(2,1)}, bf16[1024,256]{1,0:T(8,128)(2,1)}, bf16[1024,256]{1,0:T(8,128)(2,1)}) custom-call(s32[4]{0:T(128)} %pad_add_fusion.info, bf16[1,24,256,128]{3,2,1,0:T(8,128)(2,1)} %bitcast.46, bf16[1,24,256,128]{3,2,1,0:T(8,128)(2,1)} %bitcast.50, bf16[1,24,256,128]{3,2,1,0:T(8,128)(2,1)} %bitcast.54, ...), custom_call_target="tpu_custom_call" | custom-call | flops 8000000 | bytes 1 | tf_op jit(solution)/shard_map/pack/pallas_call | solution.py:281
  16.5 4.2 %pack.7 = (bf16[1280,256]{1,0:T(8,128)(2,1)}, bf16[1280,256]{1,0:T(8,128)(2,1)}, bf16[1280,256]{1,0:T(8,128)(2,1)}, bf16[1280,256]{1,0:T(8,128)(2,1)}) custom-call(s32[4]{0:T(128)} %pad_add_fusion.info, bf16[1,24,256,128]{3,2,1,0:T(8,128)(2,1)} %bitcast.47, bf16[1,24,256,128]{3,2,1,0:T(8,128)(2,1)} %bitcast.51, bf16[1,24,256,128]{3,2,1,0:T(8,128)(2,1)} %bitcast.55, ...), custom_call_target="tpu_custom_call" | custom-call | flops 10000000 | bytes 1 | tf_op jit(solution)/shard_map/pack/pallas_call | solution.py:281
  20.6 4.3 %collective-permute-done.1.refs_1_ = bf16[768,256]{1,0:T(8,128)(2,1)S(1)} collective-permute-done((bf16[768,256]{1,0:T(8,128)(2,1)}, bf16[768,256]{1,0:T(8,128)(2,1)S(1)}, u32[]{:S(2)}, u32[]{:S(2)}) %collective-permute-start.1) | collective-permute-done | bytes 393248 | tf_op jit(solution)/shard_map/ppermute | solution.py:263
  25.0 1.5 collective-permute-done.2.refs_2_
  26.5 1.1 copy-done.4
  29.0 1.5 collective-permute-start.7
  30.6 1.2 collective-permute-start.8
  31.8 7.8 %attend.4 = (bf16[1792,256]{1,0:T(8,128)(2,1)S(1)}, bf16[1792,256]{1,0:T(8,128)(2,1)S(1)}, bf16[1792,256]{1,0:T(8,128)(2,1)S(1)}, bf16[1792,256]{1,0:T(8,128)(2,...) custom-call(s32[4]{0:T(128)S(1)} %copy-done.17, bf16[1280,256]{1,0:T(8,128)(2,1)S(1)} %copy-done.18, ...), custom_call_target="tpu_custom_call" | custom-call | flops 8000000000 | bytes 1 | tf_op jit(solution)/shard_map/attend/pallas_call | solution.py:281
  39.6 3.4 %collective-permute-done.7.refs_4_.refs_9_ = bf16[512,256]{1,0:T(8,128)(2,1)S(1)} collective-permute-done((bf16[512,256]{1,0:T(8,128)(2,1)S(1)}, bf16[512,256]{1,0:T(8,128)(2,1)S(1)}, u32[]{:S(2)}, u32[]{:S(2)}) %collective-permute-start.7) | collective-permute-done | bytes 262176 | tf_op jit(solution)/shard_map/ppermute | solution.py:263
  43.1 1.3 collective-permute-start.9
  45.2 1.4 collective-permute-start.11
  46.6 15.5 %attend.5 = (bf16[1792,256]{1,0:T(8,128)(2,1)S(1)}, bf16[1792,256]{1,0:T(8,128)(2,1)S(1)}, bf16[1792,256]{1,0:T(8,128)(2,1)S(1)}, bf16[1792,256]{1,0:T(8,128)(2,...) custom-call(s32[4]{0:T(128)S(1)} %copy-done.17, ...), custom_call_target="tpu_custom_call", output_to_operand_aliasing={{0}: (13, {}), {1}: (14, {}), {2}: (15, {}), {3}: (16, {})} | custom-call | flops 16000000000 | bytes 1 | tf_op jit(solution)/shard_map/attend/pallas_call | solution.py:281
  62.1 6.6 %collective-permute-done.10.refs_4_.refs_9_ = bf16[1024,256]{1,0:T(8,128)(2,1)S(1)} collective-permute-done((bf16[1024,256]{1,0:T(8,128)(2,1)S(1)}, bf16[1024,256]{1,0:T(8,128)(2,1)S(1)}, u32[]{:S(2)}, u32[]{:S(2)}) %collective-permute-start.10) | collective-permute-done | bytes 524320 | tf_op jit(solution)/shard_map/ppermute | solution.py:263
  69.5 1.2 collective-permute-start.13
  70.7 1.7 collective-permute-start.14
  72.4 29.7 %attend.6 = (bf16[1792,256]{1,0:T(8,128)(2,1)S(1)}, bf16[1792,256]{1,0:T(8,128)(2,1)S(1)}, bf16[1792,256]{1,0:T(8,128)(2,1)S(1)}, bf16[1792,256]{1,0:T(8,128)(2,...) custom-call(s32[4]{0:T(128)S(1)} %copy-done.17, ...), custom_call_target="tpu_custom_call", output_to_operand_aliasing={{0}: (13, {}), {1}: (14, {}), {2}: (15, {}), {3}: (16, {})} | custom-call | flops 32000000000 | bytes 1 | tf_op jit(solution)/shard_map/attend/pallas_call | solution.py:281
  102.8 1.2 collective-permute-start.19
  103.9 1.7 collective-permute-start.20
  105.7 37.0 %attend.7 = (bf16[1280,256]{1,0:T(8,128)(2,1)S(1)}, bf16[1280,256]{1,0:T(8,128)(2,1)}, bf16[1280,256]{1,0:T(8,128)(2,1)}, bf16[1280,256]{1,0:T(8,128)(2,1)}, bf1...) custom-call(s32[4]{0:T(128)S(1)} %copy-done.17, ...), custom_call_target="tpu_custom_call" | custom-call | flops 40000000000 | bytes 1 | tf_op jit(solution)/shard_map/attend/pallas_call | solution.py:281
  143.5 2.7 %collective-permute-done.21 = bf16[4,1024,128]{2,1,0:T(8,128)(2,1)S(1)} collective-permute-done((bf16[4,1024,128]{2,1,0:T(8,128)(2,1)S(1)}, bf16[4,1024,128]{2,1,0:T(8,128)(2,1)S(1)}, u32[]{:S(2)}, u32[]{:S(2)}) %collective-permute-start.21) | collective-permute-done | bytes 1048608 | tf_op jit(solution)/shard_map/ppermute | solution.py:266
  146.9 3.5 %collective-permute-start.23 = (bf16[1024,128]{1,0:T(8,128)(2,1)S(1)}, bf16[1024,128]{1,0:T(8,128)(2,1)S(1)}, u32[]{:S(2)}, u32[]{:S(2)}) collective-permute-start(bf16[1024,128]{1,0:T(8,128)(2,1)S(1)} %get-tuple-element.127), channel_id=1, source_target_pairs={{0,16},{4,20},{8,24},{12,28},{16,0},{20,4},{24,8},{28,12},{1,17},{... | collective-permute-start | bytes 786440 | tf_op jit(solution)/shard_map/ppermute | solution.py:443
  151.0 1.2 collective-permute-start.16
  152.1 14.7 %collective-permute-done.24 = bf16[1024,128]{1,0:T(8,128)(2,1)S(1)} collective-permute-done((bf16[1024,128]{1,0:T(8,128)(2,1)S(1)}, bf16[1024,128]{1,0:T(8,128)(2,1)S(1)}, u32[]{:S(2)}, u32[]{:S(2)}) %collective-permute-start.24) | collective-permute-done | bytes 262176 | tf_op jit(solution)/shard_map/ppermute | solution.py:443
  166.8 1.2 collective-permute-start.17
  168.0 4.4 %unpack.2 = (bf16[1,24,256,128]{3,2,1,0:T(8,128)(2,1)}, bf16[1,24,256,128]{3,2,1,0:T(8,128)(2,1)}, bf16[1,24,256,128]{3,2,1,0:T(8,128)(2,1)}, bf16[1,24,256,128]{3,2,1,0:T(8,128)(2,1)}, f32[8,128]{1,0:T(8,128)S(1)}) custom-call(s32[4]{0:T(128)S(1)} %copy-done.17, bf16[1,24,256,128]{3,2,1,0:T(8,128)(2,1)S(1)} %bitcast.36, ...), custom_call_target="tpu_custom_call" | custom-call | flops 1 | bytes 1 | tf_op jit(solution)/shard_map/unpack/pallas_call | solution.py:281
  174.6 4.2 %all-to-all-start = ((bf16[4,256,128]{1,2,0:T(8,128)(2,1)}), bf16[4,256,128]{1,2,0:T(8,128)(2,1)S(1)}, u32[]{:S(2)}, u32[]{:S(2)}) async-start(bf16[4,256,128]{1,2,0:T(8,128)(2,1)} %copy.37), calls=%async_computation | async-start | bytes 524288 | tf_op jit(solution)/shard_map/all_to_all | solution.py:445
  178.8 5.9 %collective-permute-done.17.refs_3_ = bf16[1280,256]{1,0:T(8,128)(2,1)} collective-permute-done((bf16[1280,256]{1,0:T(8,128)(2,1)}, bf16[1280,256]{1,0:T(8,128)(2,1)}, u32[]{:S(2)}, u32[]{:S(2)}) %collective-permute-start.17) | collective-permute-done | bytes 655392 | tf_op jit(solution)/shard_map/ppermute | solution.py:263
  185.8 3.8 %unpack.3 = (bf16[1,24,256,128]{3,2,1,0:T(8,128)(2,1)}, bf16[1,24,256,128]{3,2,1,0:T(8,128)(2,1)}, bf16[1,24,256,128]{3,2,1,0:T(8,128)(2,1)}, bf16[1,24,256,128]{3,2,1,0:T(8,128)(2,1)}, f32[8,128]{1,0:T(8,128)}) custom-call(s32[4]{0:T(128)S(1)} %copy-done.17, ...), custom_call_target="tpu_custom_call", output_to_operand_aliasing={{0}: (7, {}), {1}: (8, {}), {2}: (9, {}), {3}: (10, {})} | custom-call | flops 1 | bytes 1 | tf_op jit(solution)/shard_map/unpack/pallas_call | solution.py:281
  (79 shorter events, 11.1 us)
Async XLA Ops:
  6.0 14.6 %collective-permute-start = (bf16[768,256]{1,0:T(8,128)(2,1)}, bf16[768,256]{1,0:T(8,128)(2,1)S(1)}, u32[]{:S(2)}, u32[]{:S(2)}) collective-permute-start(bf16[768,256]{1,0:T(8,128)(2,1)} %get-tuple-element.66), channel_id=1, source_target_pairs={{0,1},{1,0},{2,3},{3,2},{4,5},{5,4},{6,7},{7,6},{8,9},{9,8},{10,11... | collective-permute-start | bytes 1179656 | tf_op jit(solution)/shard_map/ppermute | solution.py:263
  6.6 18.4 %collective-permute-start.1 = (bf16[768,256]{1,0:T(8,128)(2,1)}, bf16[768,256]{1,0:T(8,128)(2,1)S(1)}, u32[]{:S(2)}, u32[]{:S(2)}) collective-permute-start(bf16[768,256]{1,0:T(8,128)(2,1)} %get-tuple-element.67), channel_id=1, source_target_pairs={{0,2},{1,3},{2,0},{3,1},{4,6},{5,7},{6,4},{7,5},{8,10},{9,11},{10,... | collective-permute-start | bytes 1179656 | tf_op jit(solution)/shard_map/ppermute | solution.py:263
  8.1 18.4 %collective-permute-start.2 = (bf16[768,256]{1,0:T(8,128)(2,1)}, bf16[768,256]{1,0:T(8,128)(2,1)S(1)}, u32[]{:S(2)}, u32[]{:S(2)}) collective-permute-start(bf16[768,256]{1,0:T(8,128)(2,1)} %get-tuple-element.68), channel_id=1, source_target_pairs={{0,3},{1,2},{2,1},{3,0},{4,7},{5,6},{6,5},{7,4},{8,11},{9,10},{10,... | collective-permute-start | bytes 1179656 | tf_op jit(solution)/shard_map/ppermute | solution.py:263
  27.6 3.0 %collective-permute-start.3 = (bf16[768,256]{1,0:T(8,128)(2,1)S(1)}, bf16[768,256]{1,0:T(8,128)(2,1)S(1)}, u32[]{:S(2)}, u32[]{:S(2)}) collective-permute-start(bf16[768,256]{1,0:T(8,128)(2,1)S(1)} %get-tuple-element.72.refs_3_.refs_1_.refs_8_), channel_id=1, source_target_pairs={{0,4},{4,0},{8,12},{12,8},{16,20},{20,16},{24,28},{28,24},{1,5},{5... | collective-permute-start | bytes 1179656 | tf_op jit(solution)/shard_map/ppermute | solution.py:266
  27.6 4.2 %collective-permute-start.4 = (bf16[768,256]{1,0:T(8,128)(2,1)S(1)}, bf16[768,256]{1,0:T(8,128)(2,1)S(1)}, u32[]{:S(2)}, u32[]{:S(2)}) collective-permute-start(bf16[768,256]{1,0:T(8,128)(2,1)S(1)} %get-tuple-element.73.refs_4_.refs_2_.refs_9_), channel_id=1, source_target_pairs={{0,4},{4,0},{8,12},{12,8},{16,20},{20,16},{24,28},{28,24},{1,5},{5... | collective-permute-start | bytes 1179656 | tf_op jit(solution)/shard_map/ppermute | solution.py:266
  28.1 3.7 %collective-permute-start.5 = (bf16[768,256]{1,0:T(8,128)(2,1)S(1)}, bf16[768,256]{1,0:T(8,128)(2,1)S(1)}, u32[]{:S(2)}, u32[]{:S(2)}) collective-permute-start(bf16[768,256]{1,0:T(8,128)(2,1)S(1)} %get-tuple-element.74.refs_5_.refs_3_.refs_10_), channel_id=1, source_target_pairs={{0,4},{4,0},{8,12},{12,8},{16,20},{20,16},{24,28},{28,24},{1,5},{5... | collective-permute-start | bytes 1179656 | tf_op jit(solution)/shard_map/ppermute | solution.py:266
  28.2 11.4 %collective-permute-start.6 = (bf16[512,256]{1,0:T(8,128)(2,1)S(1)}, bf16[512,256]{1,0:T(8,128)(2,1)S(1)}, u32[]{:S(2)}, u32[]{:S(2)}) collective-permute-start(bf16[512,256]{1,0:T(8,128)(2,1)S(1)} %get-tuple-element.84), channel_id=1, source_target_pairs={{0,1},{1,0},{2,3},{3,2},{4,5},{5,4},{6,7},{7,6},{8,9},{9,8},{10,11... | collective-permute-start | bytes 786440 | tf_op jit(solution)/shard_map/ppermute | solution.py:263
  29.0 14.0 %collective-permute-start.7 = (bf16[512,256]{1,0:T(8,128)(2,1)S(1)}, bf16[512,256]{1,0:T(8,128)(2,1)S(1)}, u32[]{:S(2)}, u32[]{:S(2)}) collective-permute-start(bf16[512,256]{1,0:T(8,128)(2,1)S(1)} %get-tuple-element.85), channel_id=1, source_target_pairs={{0,2},{1,3},{2,0},{3,1},{4,6},{5,7},{6,4},{7,5},{8,10},{9,11},{10,... | collective-permute-start | bytes 786440 | tf_op jit(solution)/shard_map/ppermute | solution.py:263
  30.6 12.5 %collective-permute-start.8 = (bf16[512,256]{1,0:T(8,128)(2,1)S(1)}, bf16[512,256]{1,0:T(8,128)(2,1)S(1)}, u32[]{:S(2)}, u32[]{:S(2)}) collective-permute-start(bf16[512,256]{1,0:T(8,128)(2,1)S(1)} %get-tuple-element.86), channel_id=1, source_target_pairs={{0,3},{1,2},{2,1},{3,0},{4,7},{5,6},{6,5},{7,4},{8,11},{9,10},{10,... | collective-permute-start | bytes 786440 | tf_op jit(solution)/shard_map/ppermute | solution.py:263
  43.1 19.1 %collective-permute-start.9 = (bf16[1024,256]{1,0:T(8,128)(2,1)S(1)}, bf16[1024,256]{1,0:T(8,128)(2,1)S(1)}, u32[]{:S(2)}, u32[]{:S(2)}) collective-permute-start(bf16[1024,256]{1,0:T(8,128)(2,1)S(1)} %get-tuple-element.88), channel_id=1, source_target_pairs={{0,1},{1,0},{2,3},{3,2},{4,5},{5,4},{6,7},{7,6},{8,9},{9,8},{10,11... | collective-permute-start | bytes 1572872 | tf_op jit(solution)/shard_map/ppermute | solution.py:263
  44.4 24.4 %collective-permute-start.10 = (bf16[1024,256]{1,0:T(8,128)(2,1)S(1)}, bf16[1024,256]{1,0:T(8,128)(2,1)S(1)}, u32[]{:S(2)}, u32[]{:S(2)}) collective-permute-start(bf16[1024,256]{1,0:T(8,128)(2,1)S(1)} %get-tuple-element.89), channel_id=1, source_target_pairs={{0,2},{1,3},{2,0},{3,1},{4,6},{5,7},{6,4},{7,5},{8,10},{9,11},{10,... | collective-permute-start | bytes 1572872 | tf_op jit(solution)/shard_map/ppermute | solution.py:263
  45.2 23.6 %collective-permute-start.11 = (bf16[1024,256]{1,0:T(8,128)(2,1)S(1)}, bf16[1024,256]{1,0:T(8,128)(2,1)S(1)}, u32[]{:S(2)}, u32[]{:S(2)}) collective-permute-start(bf16[1024,256]{1,0:T(8,128)(2,1)S(1)} %get-tuple-element.90), channel_id=1, source_target_pairs={{0,3},{1,2},{2,1},{3,0},{4,7},{5,6},{6,5},{7,4},{8,11},{9,10},{10,... | collective-permute-start | bytes 1572872 | tf_op jit(solution)/shard_map/ppermute | solution.py:263
  46.6 22.2 %copy-start.6 = (bf16[1280,256]{1,0:T(8,128)(2,1)S(1)}, bf16[1280,256]{1,0:T(8,128)(2,1)}, u32[]{:S(2)}) copy-start(bf16[1280,256]{1,0:T(8,128)(2,1)} %get-tuple-element.75.refs_0_) | copy-start | bytes 1966084
  46.6 22.2 %copy-start.7 = (bf16[1280,256]{1,0:T(8,128)(2,1)S(1)}, bf16[1280,256]{1,0:T(8,128)(2,1)}, u32[]{:S(2)}) copy-start(bf16[1280,256]{1,0:T(8,128)(2,1)} %get-tuple-element.76.refs_1_) | copy-start | bytes 1966084
  46.6 22.2 %copy-start.8 = (bf16[1280,256]{1,0:T(8,128)(2,1)S(1)}, bf16[1280,256]{1,0:T(8,128)(2,1)}, u32[]{:S(2)}) copy-start(bf16[1280,256]{1,0:T(8,128)(2,1)} %get-tuple-element.77.refs_2_) | copy-start | bytes 1966084
  68.8 35.1 %collective-permute-start.12 = (bf16[1280,256]{1,0:T(8,128)(2,1)S(1)}, bf16[1280,256]{1,0:T(8,128)(2,1)S(1)}, u32[]{:S(2)}, u32[]{:S(2)}) collective-permute-start(bf16[1280,256]{1,0:T(8,128)(2,1)S(1)} %get-tuple-element.97), channel_id=1, source_target_pairs={{0,1},{1,0},{2,3},{3,2},{4,5},{5,4},{6,7},{7,6},{8,9},{9,8},{10,11... | collective-permute-start | bytes 1966088 | tf_op jit(solution)/shard_map/ppermute | solution.py:263
  69.5 36.2 %collective-permute-start.13 = (bf16[1280,256]{1,0:T(8,128)(2,1)S(1)}, bf16[1280,256]{1,0:T(8,128)(2,1)S(1)}, u32[]{:S(2)}, u32[]{:S(2)}) collective-permute-start(bf16[1280,256]{1,0:T(8,128)(2,1)S(1)} %get-tuple-element.98), channel_id=1, source_target_pairs={{0,2},{1,3},{2,0},{3,1},{4,6},{5,7},{6,4},{7,5},{8,10},{9,11},{10,... | collective-permute-start | bytes 1966088 | tf_op jit(solution)/shard_map/ppermute | solution.py:263
  70.7 35.0 %collective-permute-start.14 = (bf16[1280,256]{1,0:T(8,128)(2,1)S(1)}, bf16[1280,256]{1,0:T(8,128)(2,1)S(1)}, u32[]{:S(2)}, u32[]{:S(2)}) collective-permute-start(bf16[1280,256]{1,0:T(8,128)(2,1)S(1)} %get-tuple-element.99), channel_id=1, source_target_pairs={{0,3},{1,2},{2,1},{3,0},{4,7},{5,6},{6,5},{7,4},{8,11},{9,10},{10,... | collective-permute-start | bytes 1966088 | tf_op jit(solution)/shard_map/ppermute | solution.py:263
  72.4 33.3 %copy-start.5 = (bf16[1280,256]{1,0:T(8,128)(2,1)S(1)}, bf16[1280,256]{1,0:T(8,128)(2,1)}, u32[]{:S(2)}) copy-start(bf16[1280,256]{1,0:T(8,128)(2,1)} %get-tuple-element.71.refs_5_.refs_7_) | copy-start | bytes 1966084
  102.1 40.6 %collective-permute-start.18 = (bf16[1792,256]{1,0:T(8,128)(2,1)S(1)}, bf16[1792,256]{1,0:T(8,128)(2,1)S(1)}, u32[]{:S(2)}, u32[]{:S(2)}) collective-permute-start(bf16[1792,256]{1,0:T(8,128)(2,1)S(1)} %get-tuple-element.111), channel_id=1, source_target_pairs={{0,1},{1,0},{2,3},{3,2},{4,5},{5,4},{6,7},{7,6},{8,9},{9,8},{10,11... | collective-permute-start | bytes 2752520 | tf_op jit(solution)/shard_map/ppermute | solution.py:263
  102.8 39.9 %collective-permute-start.19 = (bf16[1792,256]{1,0:T(8,128)(2,1)S(1)}, bf16[1792,256]{1,0:T(8,128)(2,1)S(1)}, u32[]{:S(2)}, u32[]{:S(2)}) collective-permute-start(bf16[1792,256]{1,0:T(8,128)(2,1)S(1)} %get-tuple-element.112), channel_id=1, source_target_pairs={{0,2},{1,3},{2,0},{3,1},{4,6},{5,7},{6,4},{7,5},{8,10},{9,11},{10,... | collective-permute-start | bytes 2752520 | tf_op jit(solution)/shard_map/ppermute | solution.py:263
  103.9 38.7 %collective-permute-start.20 = (bf16[1792,256]{1,0:T(8,128)(2,1)S(1)}, bf16[1792,256]{1,0:T(8,128)(2,1)S(1)}, u32[]{:S(2)}, u32[]{:S(2)}) collective-permute-start(bf16[1792,256]{1,0:T(8,128)(2,1)S(1)} %get-tuple-element.113), channel_id=1, source_target_pairs={{0,3},{1,2},{2,1},{3,0},{4,7},{5,6},{6,5},{7,4},{8,11},{9,10},{10,... | collective-permute-start | bytes 2752520 | tf_op jit(solution)/shard_map/ppermute | solution.py:263
  142.7 25.3 %copy-start.1 = (bf16[24,256,128]{2,1,0:T(8,128)(2,1)S(1)}, bf16[24,256,128]{2,1,0:T(8,128)(2,1)}, u32[]{:S(2)}) copy-start(bf16[24,256,128]{2,1,0:T(8,128)(2,1)} %param.11) | copy-start | bytes 4718596
  143.5 24.5 %copy-start = (bf16[24,256,128]{2,1,0:T(8,128)(2,1)S(1)}, bf16[24,256,128]{2,1,0:T(8,128)(2,1)}, u32[]{:S(2)}) copy-start(bf16[24,256,128]{2,1,0:T(8,128)(2,1)} %param.10) | copy-start | bytes 4718596
  143.5 2.7 %collective-permute-start.21 = (bf16[4,1024,128]{2,1,0:T(8,128)(2,1)S(1)}, bf16[4,1024,128]{2,1,0:T(8,128)(2,1)S(1)}, u32[]{:S(2)}, u32[]{:S(2)}) collective-permute-start(bf16[4,1024,128]{2,1,0:T(8,128)(2,1)S(1)} %hold.9), channel_id=1, source_target_pairs={{0,4},{4,0},{8,12},{12,8},{16,20},{20,16},{24,28},{28,24},{1,5},{5... | collective-permute-start | bytes 3145736 | tf_op jit(solution)/shard_map/ppermute | solution.py:266
  146.4 20.4 %collective-permute-start.24 = (bf16[1024,128]{1,0:T(8,128)(2,1)S(1)}, bf16[1024,128]{1,0:T(8,128)(2,1)S(1)}, u32[]{:S(2)}, u32[]{:S(2)}) collective-permute-start(bf16[1024,128]{1,0:T(8,128)(2,1)S(1)} %get-tuple-element.126), channel_id=1, source_target_pairs={{0,24},{4,28},{8,16},{12,20},{16,8},{20,12},{24,0},{28,4},{1,25},{... | collective-permute-start | bytes 786440 | tf_op jit(solution)/shard_map/ppermute | solution.py:443
  146.9 26.0 %collective-permute-start.23 = (bf16[1024,128]{1,0:T(8,128)(2,1)S(1)}, bf16[1024,128]{1,0:T(8,128)(2,1)S(1)}, u32[]{:S(2)}, u32[]{:S(2)}) collective-permute-start(bf16[1024,128]{1,0:T(8,128)(2,1)S(1)} %get-tuple-element.127), channel_id=1, source_target_pairs={{0,16},{4,20},{8,24},{12,28},{16,0},{20,4},{24,8},{28,12},{1,17},{... | collective-permute-start | bytes 786440 | tf_op jit(solution)/shard_map/ppermute | solution.py:443
  150.4 22.5 %collective-permute-start.22 = (bf16[1024,128]{1,0:T(8,128)(2,1)S(1)}, bf16[1024,128]{1,0:T(8,128)(2,1)S(1)}, u32[]{:S(2)}, u32[]{:S(2)}) collective-permute-start(bf16[1024,128]{1,0:T(8,128)(2,1)S(1)} %get-tuple-element.125), channel_id=1, source_target_pairs={{0,8},{4,12},{8,0},{12,4},{16,24},{20,28},{24,16},{28,20},{1,9},{5... | collective-permute-start | bytes 786440 | tf_op jit(solution)/shard_map/ppermute | solution.py:443
  150.4 28.4 %collective-permute-start.15 = (bf16[1280,256]{1,0:T(8,128)(2,1)}, bf16[1280,256]{1,0:T(8,128)(2,1)}, u32[]{:S(2)}, u32[]{:S(2)}) collective-permute-start(bf16[1280,256]{1,0:T(8,128)(2,1)} %get-tuple-element.107), channel_id=1, source_target_pairs={{0,1},{1,0},{2,3},{3,2},{4,5},{5,4},{6,7},{7,6},{8,9},{9,8},{10,11... | collective-permute-start | bytes 1966088 | tf_op jit(solution)/shard_map/ppermute | solution.py:263
  151.0 27.8 %collective-permute-start.16 = (bf16[1280,256]{1,0:T(8,128)(2,1)}, bf16[1280,256]{1,0:T(8,128)(2,1)}, u32[]{:S(2)}, u32[]{:S(2)}) collective-permute-start(bf16[1280,256]{1,0:T(8,128)(2,1)} %get-tuple-element.108), channel_id=1, source_target_pairs={{0,2},{1,3},{2,0},{3,1},{4,6},{5,7},{6,4},{7,5},{8,10},{9,11},{10,... | collective-permute-start | bytes 1966088 | tf_op jit(solution)/shard_map/ppermute | solution.py:263
  166.8 17.9 %collective-permute-start.17 = (bf16[1280,256]{1,0:T(8,128)(2,1)}, bf16[1280,256]{1,0:T(8,128)(2,1)}, u32[]{:S(2)}, u32[]{:S(2)}) collective-permute-start(bf16[1280,256]{1,0:T(8,128)(2,1)} %get-tuple-element.109), channel_id=1, source_target_pairs={{0,3},{1,2},{2,1},{3,0},{4,7},{5,6},{6,5},{7,4},{8,11},{9,10},{10,... | collective-permute-start | bytes 1966088 | tf_op jit(solution)/shard_map/ppermute | solution.py:263
  174.6 15.1 %all-to-all-start = ((bf16[4,256,128]{1,2,0:T(8,128)(2,1)}), bf16[4,256,128]{1,2,0:T(8,128)(2,1)S(1)}, u32[]{:S(2)}, u32[]{:S(2)}) async-start(bf16[4,256,128]{1,2,0:T(8,128)(2,1)} %copy.37), calls=%async_computation | async-start | bytes 524288 | tf_op jit(solution)/shard_map/all_to_all | solution.py:445
  (13 other events, 100.5 us)

commit v2 on v1

--- a/solution.py
+++ b/solution.py
@@ -194,13 +194,15 @@
         return [functools.partial(step, jb, *at) for at in itertools.product(*ranges)]
 
     def finish(jb):
-        return each(value_grad, jb, some) + each(query_grad, jb, some) + each(key_grad, jb, some)
-
+        return each(query_grad, jb, some) + each(key_grad, jb, some)
+
+    early, late = tiles[: len(tiles) // 2], tiles[len(tiles) // 2 :]
     woven(each(score, 0, some, tiles))
     for jb in range(n_col):
-        woven(each(expand, jb, some, tiles), finish(jb - 1))
-        woven(each(attend, jb, some), each(score, jb + 1, some, tiles[: len(tiles) // 2]))
-        woven(each(back, jb, tiles), each(score, jb + 1, some, tiles[len(tiles) // 2 :]))
+        ahead = each(score, jb + 1, some, early)
+        woven(each(expand, jb, some, tiles), finish(jb - 1) if jb else ahead)
+        woven(each(attend, jb, some), ahead if jb else [])
+        woven(each(back, jb, tiles), each(score, jb + 1, some, late), each(value_grad, jb, some))
     woven(finish(n_col - 1))
 
     for r in some:

time: 192 us -> 191 us (level)
  no operation moved by 1% of the time
where the time goes in v2:
time: 191 us; the launch traced here: 190 us
  Pallas kernels  113 us (59%)
  waiting for transfers between devices  39.5 us (21%)
  starting transfers between devices  29.5 us (15%)
  local copies, waits for them, and re-layouts  4.4 us (2%)
  other arithmetic  2.49 us (1%)
    pallas_call x10, Pallas kernels, call(): pl.pallas_call(kernel, grid_spec=pltpu.PrefetchScalarGridSpec(num_scalar_...  113 us
    ppermute x18, waiting for transfers between devices, exchange(): lax.ppermute(blocks[step], 'col', pairs[step])  22.1 us
    ppermute x18, starting transfers between devices, exchange(): lax.ppermute(blocks[step], 'col', pairs[step])  20.7 us
    ppermute x3, waiting for transfers between devices, on_device(): lax.ppermute(share.astype(jnp.bfloat16), 'row', pairs).astype(jnp.float32)  14.7 us
    all_to_all x1, starting transfers between devices, on_device(): lax.all_to_all(total, 'col', split_axis=0, concat_axis=0, tiled=True)  4.16 us
    ppermute x3, starting transfers between devices, on_device(): lax.ppermute(share.astype(jnp.bfloat16), 'row', pairs).astype(jnp.float32)  4.01 us
  transfers between devices with their start and end apart: 26, of which 7 were waited for; matrix products, arithmetic and copies ran while one was open for 1% of the time, Pallas kernels for 57%

profile of v2, /device:TPU:18, one launch (start us, length us, event | category | flops | bytes accessed | tf_op | source)
XLA Modules:
  0.0 190.0 jit_solution(8412642369400820384)
XLA Ops:
  1.9 4.1 %pack.4 = (bf16[1280,256]{1,0:T(8,128)(2,1)}, bf16[768,256]{1,0:T(8,128)(2,1)}, bf16[768,256]{1,0:T(8,128)(2,1)}, bf16[768,256]{1,0:T(8,128)(2,1)}) custom-call(s32[4]{0:T(128)} %pad_add_fusion.info, bf16[1,24,256,128]{3,2,1,0:T(8,128)(2,1)} %bitcast.44, bf16[1,24,256,128]{3,2,1,0:T(8,128)(2,1)} %bitcast.48, bf16[1,24,256,128]{3,2,1,0:T(8,128)(2,1)} %bitcast.52, ...), custom_call_target="tpu_custom_call" | custom-call | flops 2000000 | bytes 1 | tf_op jit(solution)/shard_map/pack/pallas_call | solution.py:283
  6.6 1.5 collective-permute-start.1
  8.1 1.4 collective-permute-start.2
  9.5 3.2 %pack.5 = (bf16[512,256]{1,0:T(8,128)(2,1)}, bf16[512,256]{1,0:T(8,128)(2,1)}, bf16[512,256]{1,0:T(8,128)(2,1)}, bf16[512,256]{1,0:T(8,128)(2,1)}) custom-call(s32[4]{0:T(128)} %pad_add_fusion.info, bf16[1,24,256,128]{3,2,1,0:T(8,128)(2,1)} %bitcast.45, bf16[1,24,256,128]{3,2,1,0:T(8,128)(2,1)} %bitcast.49, bf16[1,24,256,128]{3,2,1,0:T(8,128)(2,1)} %bitcast.53, ...), custom_call_target="tpu_custom_call" | custom-call | flops 4000000 | bytes 1 | tf_op jit(solution)/shard_map/pack/pallas_call | solution.py:283
  12.8 3.7 %pack.6 = (bf16[1024,256]{1,0:T(8,128)(2,1)}, bf16[1024,256]{1,0:T(8,128)(2,1)}, bf16[1024,256]{1,0:T(8,128)(2,1)}, bf16[1024,256]{1,0:T(8,128)(2,1)}) custom-call(s32[4]{0:T(128)} %pad_add_fusion.info, bf16[1,24,256,128]{3,2,1,0:T(8,128)(2,1)} %bitcast.46, bf16[1,24,256,128]{3,2,1,0:T(8,128)(2,1)} %bitcast.50, bf16[1,24,256,128]{3,2,1,0:T(8,128)(2,1)} %bitcast.54, ...), custom_call_target="tpu_custom_call" | custom-call | flops 8000000 | bytes 1 | tf_op jit(solution)/shard_map/pack/pallas_call | solution.py:283
  16.5 4.2 %pack.7 = (bf16[1280,256]{1,0:T(8,128)(2,1)}, bf16[1280,256]{1,0:T(8,128)(2,1)}, bf16[1280,256]{1,0:T(8,128)(2,1)}, bf16[1280,256]{1,0:T(8,128)(2,1)}) custom-call(s32[4]{0:T(128)} %pad_add_fusion.info, bf16[1,24,256,128]{3,2,1,0:T(8,128)(2,1)} %bitcast.47, bf16[1,24,256,128]{3,2,1,0:T(8,128)(2,1)} %bitcast.51, bf16[1,24,256,128]{3,2,1,0:T(8,128)(2,1)} %bitcast.55, ...), custom_call_target="tpu_custom_call" | custom-call | flops 10000000 | bytes 1 | tf_op jit(solution)/shard_map/pack/pallas_call | solution.py:283
  20.6 4.3 %collective-permute-done.1.refs_1_ = bf16[768,256]{1,0:T(8,128)(2,1)S(1)} collective-permute-done((bf16[768,256]{1,0:T(8,128)(2,1)}, bf16[768,256]{1,0:T(8,128)(2,1)S(1)}, u32[]{:S(2)}, u32[]{:S(2)}) %collective-permute-start.1) | collective-permute-done | bytes 393248 | tf_op jit(solution)/shard_map/ppermute | solution.py:265
  25.0 1.5 collective-permute-done.2.refs_2_
  26.5 1.1 copy-done.4
  29.0 1.5 collective-permute-start.7
  30.6 1.2 collective-permute-start.8
  31.8 7.7 %attend.4 = (bf16[1792,256]{1,0:T(8,128)(2,1)S(1)}, bf16[1792,256]{1,0:T(8,128)(2,1)S(1)}, bf16[1792,256]{1,0:T(8,128)(2,1)S(1)}, bf16[1792,256]{1,0:T(8,128)(2,...) custom-call(s32[4]{0:T(128)S(1)} %copy-done.17, bf16[1280,256]{1,0:T(8,128)(2,1)S(1)} %copy-done.18, ...), custom_call_target="tpu_custom_call" | custom-call | flops 8000000000 | bytes 1 | tf_op jit(solution)/shard_map/attend/pallas_call | solution.py:283
  39.5 3.5 %collective-permute-done.7.refs_4_.refs_9_ = bf16[512,256]{1,0:T(8,128)(2,1)S(1)} collective-permute-done((bf16[512,256]{1,0:T(8,128)(2,1)S(1)}, bf16[512,256]{1,0:T(8,128)(2,1)S(1)}, u32[]{:S(2)}, u32[]{:S(2)}) %collective-permute-start.7) | collective-permute-done | bytes 262176 | tf_op jit(solution)/shard_map/ppermute | solution.py:265
  43.1 1.3 collective-permute-start.9
  45.2 1.4 collective-permute-start.11
  46.6 15.4 %attend.5 = (bf16[1792,256]{1,0:T(8,128)(2,1)S(1)}, bf16[1792,256]{1,0:T(8,128)(2,1)S(1)}, bf16[1792,256]{1,0:T(8,128)(2,1)S(1)}, bf16[1792,256]{1,0:T(8,128)(2,...) custom-call(s32[4]{0:T(128)S(1)} %copy-done.17, ...), custom_call_target="tpu_custom_call", output_to_operand_aliasing={{0}: (13, {}), {1}: (14, {}), {2}: (15, {}), {3}: (16, {})} | custom-call | flops 16000000000 | bytes 1 | tf_op jit(solution)/shard_map/attend/pallas_call | solution.py:283
  62.0 6.8 %collective-permute-done.10.refs_4_.refs_9_ = bf16[1024,256]{1,0:T(8,128)(2,1)S(1)} collective-permute-done((bf16[1024,256]{1,0:T(8,128)(2,1)S(1)}, bf16[1024,256]{1,0:T(8,128)(2,1)S(1)}, u32[]{:S(2)}, u32[]{:S(2)}) %collective-permute-start.10) | collective-permute-done | bytes 524320 | tf_op jit(solution)/shard_map/ppermute | solution.py:265
  69.5 1.2 collective-permute-start.13
  70.7 1.7 collective-permute-start.14
  72.4 29.4 %attend.6 = (bf16[1792,256]{1,0:T(8,128)(2,1)S(1)}, bf16[1792,256]{1,0:T(8,128)(2,1)S(1)}, bf16[1792,256]{1,0:T(8,128)(2,1)S(1)}, bf16[1792,256]{1,0:T(8,128)(2,...) custom-call(s32[4]{0:T(128)S(1)} %copy-done.17, ...), custom_call_target="tpu_custom_call", output_to_operand_aliasing={{0}: (13, {}), {1}: (14, {}), {2}: (15, {}), {3}: (16, {})} | custom-call | flops 32000000000 | bytes 1 | tf_op jit(solution)/shard_map/attend/pallas_call | solution.py:283
  102.5 1.2 collective-permute-start.19
  103.6 1.7 collective-permute-start.20
  105.4 36.7 %attend.7 = (bf16[1280,256]{1,0:T(8,128)(2,1)S(1)}, bf16[1280,256]{1,0:T(8,128)(2,1)}, bf16[1280,256]{1,0:T(8,128)(2,1)}, bf16[1280,256]{1,0:T(8,128)(2,1)}, bf1...) custom-call(s32[4]{0:T(128)S(1)} %copy-done.17, ...), custom_call_target="tpu_custom_call" | custom-call | flops 40000000000 | bytes 1 | tf_op jit(solution)/shard_map/attend/pallas_call | solution.py:283
  142.9 2.7 %collective-permute-done.21 = bf16[4,1024,128]{2,1,0:T(8,128)(2,1)S(1)} collective-permute-done((bf16[4,1024,128]{2,1,0:T(8,128)(2,1)S(1)}, bf16[4,1024,128]{2,1,0:T(8,128)(2,1)S(1)}, u32[]{:S(2)}, u32[]{:S(2)}) %collective-permute-start.21) | collective-permute-done | bytes 1048608 | tf_op jit(solution)/shard_map/ppermute | solution.py:268
  146.4 3.5 %collective-permute-start.23 = (bf16[1024,128]{1,0:T(8,128)(2,1)S(1)}, bf16[1024,128]{1,0:T(8,128)(2,1)S(1)}, u32[]{:S(2)}, u32[]{:S(2)}) collective-permute-start(bf16[1024,128]{1,0:T(8,128)(2,1)S(1)} %get-tuple-element.127), channel_id=1, source_target_pairs={{0,16},{4,20},{8,24},{12,28},{16,0},{20,4},{24,8},{28,12},{1,17},{... | collective-permute-start | bytes 786440 | tf_op jit(solution)/shard_map/ppermute | solution.py:445
  150.4 1.2 collective-permute-start.16
  151.6 14.6 %collective-permute-done.24 = bf16[1024,128]{1,0:T(8,128)(2,1)S(1)} collective-permute-done((bf16[1024,128]{1,0:T(8,128)(2,1)S(1)}, bf16[1024,128]{1,0:T(8,128)(2,1)S(1)}, u32[]{:S(2)}, u32[]{:S(2)}) %collective-permute-start.24) | collective-permute-done | bytes 262176 | tf_op jit(solution)/shard_map/ppermute | solution.py:445
  166.3 1.2 collective-permute-start.17
  167.5 4.4 %unpack.2 = (bf16[1,24,256,128]{3,2,1,0:T(8,128)(2,1)}, bf16[1,24,256,128]{3,2,1,0:T(8,128)(2,1)}, bf16[1,24,256,128]{3,2,1,0:T(8,128)(2,1)}, bf16[1,24,256,128]{3,2,1,0:T(8,128)(2,1)}, f32[8,128]{1,0:T(8,128)S(1)}) custom-call(s32[4]{0:T(128)S(1)} %copy-done.17, bf16[1,24,256,128]{3,2,1,0:T(8,128)(2,1)S(1)} %bitcast.36, ...), custom_call_target="tpu_custom_call" | custom-call | flops 1 | bytes 1 | tf_op jit(solution)/shard_map/unpack/pallas_call | solution.py:283
  174.1 4.2 %all-to-all-start = ((bf16[4,256,128]{1,2,0:T(8,128)(2,1)}), bf16[4,256,128]{1,2,0:T(8,128)(2,1)S(1)}, u32[]{:S(2)}, u32[]{:S(2)}) async-start(bf16[4,256,128]{1,2,0:T(8,128)(2,1)} %copy.37), calls=%async_computation | async-start | bytes 524288 | tf_op jit(solution)/shard_map/all_to_all | solution.py:447
  178.3 5.9 %collective-permute-done.17.refs_3_ = bf16[1280,256]{1,0:T(8,128)(2,1)} collective-permute-done((bf16[1280,256]{1,0:T(8,128)(2,1)}, bf16[1280,256]{1,0:T(8,128)(2,1)}, u32[]{:S(2)}, u32[]{:S(2)}) %collective-permute-start.17) | collective-permute-done | bytes 655392 | tf_op jit(solution)/shard_map/ppermute | solution.py:265
  185.3 3.8 %unpack.3 = (bf16[1,24,256,128]{3,2,1,0:T(8,128)(2,1)}, bf16[1,24,256,128]{3,2,1,0:T(8,128)(2,1)}, bf16[1,24,256,128]{3,2,1,0:T(8,128)(2,1)}, bf16[1,24,256,128]{3,2,1,0:T(8,128)(2,1)}, f32[8,128]{1,0:T(8,128)}) custom-call(s32[4]{0:T(128)S(1)} %copy-done.17, ...), custom_call_target="tpu_custom_call", output_to_operand_aliasing={{0}: (7, {}), {1}: (8, {}), {2}: (9, {}), {3}: (10, {})} | custom-call | flops 1 | bytes 1 | tf_op jit(solution)/shard_map/unpack/pallas_call | solution.py:283
  (79 shorter events, 11.1 us)
Async XLA Ops:
  6.0 14.6 %collective-permute-start = (bf16[768,256]{1,0:T(8,128)(2,1)}, bf16[768,256]{1,0:T(8,128)(2,1)S(1)}, u32[]{:S(2)}, u32[]{:S(2)}) collective-permute-start(bf16[768,256]{1,0:T(8,128)(2,1)} %get-tuple-element.66), channel_id=1, source_target_pairs={{0,1},{1,0},{2,3},{3,2},{4,5},{5,4},{6,7},{7,6},{8,9},{9,8},{10,11... | collective-permute-start | bytes 1179656 | tf_op jit(solution)/shard_map/ppermute | solution.py:265
  6.6 18.4 %collective-permute-start.1 = (bf16[768,256]{1,0:T(8,128)(2,1)}, bf16[768,256]{1,0:T(8,128)(2,1)S(1)}, u32[]{:S(2)}, u32[]{:S(2)}) collective-permute-start(bf16[768,256]{1,0:T(8,128)(2,1)} %get-tuple-element.67), channel_id=1, source_target_pairs={{0,2},{1,3},{2,0},{3,1},{4,6},{5,7},{6,4},{7,5},{8,10},{9,11},{10,... | collective-permute-start | bytes 1179656 | tf_op jit(solution)/shard_map/ppermute | solution.py:265
  8.1 18.4 %collective-permute-start.2 = (bf16[768,256]{1,0:T(8,128)(2,1)}, bf16[768,256]{1,0:T(8,128)(2,1)S(1)}, u32[]{:S(2)}, u32[]{:S(2)}) collective-permute-start(bf16[768,256]{1,0:T(8,128)(2,1)} %get-tuple-element.68), channel_id=1, source_target_pairs={{0,3},{1,2},{2,1},{3,0},{4,7},{5,6},{6,5},{7,4},{8,11},{9,10},{10,... | collective-permute-start | bytes 1179656 | tf_op jit(solution)/shard_map/ppermute | solution.py:265
  27.6 3.0 %collective-permute-start.3 = (bf16[768,256]{1,0:T(8,128)(2,1)S(1)}, bf16[768,256]{1,0:T(8,128)(2,1)S(1)}, u32[]{:S(2)}, u32[]{:S(2)}) collective-permute-start(bf16[768,256]{1,0:T(8,128)(2,1)S(1)} %get-tuple-element.72.refs_3_.refs_1_.refs_8_), channel_id=1, source_target_pairs={{0,4},{4,0},{8,12},{12,8},{16,20},{20,16},{24,28},{28,24},{1,5},{5... | collective-permute-start | bytes 1179656 | tf_op jit(solution)/shard_map/ppermute | solution.py:268
  27.6 4.2 %collective-permute-start.4 = (bf16[768,256]{1,0:T(8,128)(2,1)S(1)}, bf16[768,256]{1,0:T(8,128)(2,1)S(1)}, u32[]{:S(2)}, u32[]{:S(2)}) collective-permute-start(bf16[768,256]{1,0:T(8,128)(2,1)S(1)} %get-tuple-element.73.refs_4_.refs_2_.refs_9_), channel_id=1, source_target_pairs={{0,4},{4,0},{8,12},{12,8},{16,20},{20,16},{24,28},{28,24},{1,5},{5... | collective-permute-start | bytes 1179656 | tf_op jit(solution)/shard_map/ppermute | solution.py:268
  28.1 3.7 %collective-permute-start.5 = (bf16[768,256]{1,0:T(8,128)(2,1)S(1)}, bf16[768,256]{1,0:T(8,128)(2,1)S(1)}, u32[]{:S(2)}, u32[]{:S(2)}) collective-permute-start(bf16[768,256]{1,0:T(8,128)(2,1)S(1)} %get-tuple-element.74.refs_5_.refs_3_.refs_10_), channel_id=1, source_target_pairs={{0,4},{4,0},{8,12},{12,8},{16,20},{20,16},{24,28},{28,24},{1,5},{5... | collective-permute-start | bytes 1179656 | tf_op jit(solution)/shard_map/ppermute | solution.py:268
  28.2 11.3 %collective-permute-start.6 = (bf16[512,256]{1,0:T(8,128)(2,1)S(1)}, bf16[512,256]{1,0:T(8,128)(2,1)S(1)}, u32[]{:S(2)}, u32[]{:S(2)}) collective-permute-start(bf16[512,256]{1,0:T(8,128)(2,1)S(1)} %get-tuple-element.84), channel_id=1, source_target_pairs={{0,1},{1,0},{2,3},{3,2},{4,5},{5,4},{6,7},{7,6},{8,9},{9,8},{10,11... | collective-permute-start | bytes 786440 | tf_op jit(solution)/shard_map/ppermute | solution.py:265
  29.0 14.0 %collective-permute-start.7 = (bf16[512,256]{1,0:T(8,128)(2,1)S(1)}, bf16[512,256]{1,0:T(8,128)(2,1)S(1)}, u32[]{:S(2)}, u32[]{:S(2)}) collective-permute-start(bf16[512,256]{1,0:T(8,128)(2,1)S(1)} %get-tuple-element.85), channel_id=1, source_target_pairs={{0,2},{1,3},{2,0},{3,1},{4,6},{5,7},{6,4},{7,5},{8,10},{9,11},{10,... | collective-permute-start | bytes 786440 | tf_op jit(solution)/shard_map/ppermute | solution.py:265
  30.6 12.5 %collective-permute-start.8 = (bf16[512,256]{1,0:T(8,128)(2,1)S(1)}, bf16[512,256]{1,0:T(8,128)(2,1)S(1)}, u32[]{:S(2)}, u32[]{:S(2)}) collective-permute-start(bf16[512,256]{1,0:T(8,128)(2,1)S(1)} %get-tuple-element.86), channel_id=1, source_target_pairs={{0,3},{1,2},{2,1},{3,0},{4,7},{5,6},{6,5},{7,4},{8,11},{9,10},{10,... | collective-permute-start | bytes 786440 | tf_op jit(solution)/shard_map/ppermute | solution.py:265
  43.1 18.9 %collective-permute-start.9 = (bf16[1024,256]{1,0:T(8,128)(2,1)S(1)}, bf16[1024,256]{1,0:T(8,128)(2,1)S(1)}, u32[]{:S(2)}, u32[]{:S(2)}) collective-permute-start(bf16[1024,256]{1,0:T(8,128)(2,1)S(1)} %get-tuple-element.88), channel_id=1, source_target_pairs={{0,1},{1,0},{2,3},{3,2},{4,5},{5,4},{6,7},{7,6},{8,9},{9,8},{10,11... | collective-permute-start | bytes 1572872 | tf_op jit(solution)/shard_map/ppermute | solution.py:265
  44.4 24.4 %collective-permute-start.10 = (bf16[1024,256]{1,0:T(8,128)(2,1)S(1)}, bf16[1024,256]{1,0:T(8,128)(2,1)S(1)}, u32[]{:S(2)}, u32[]{:S(2)}) collective-permute-start(bf16[1024,256]{1,0:T(8,128)(2,1)S(1)} %get-tuple-element.89), channel_id=1, source_target_pairs={{0,2},{1,3},{2,0},{3,1},{4,6},{5,7},{6,4},{7,5},{8,10},{9,11},{10,... | collective-permute-start | bytes 1572872 | tf_op jit(solution)/shard_map/ppermute | solution.py:265
  45.2 23.6 %collective-permute-start.11 = (bf16[1024,256]{1,0:T(8,128)(2,1)S(1)}, bf16[1024,256]{1,0:T(8,128)(2,1)S(1)}, u32[]{:S(2)}, u32[]{:S(2)}) collective-permute-start(bf16[1024,256]{1,0:T(8,128)(2,1)S(1)} %get-tuple-element.90), channel_id=1, source_target_pairs={{0,3},{1,2},{2,1},{3,0},{4,7},{5,6},{6,5},{7,4},{8,11},{9,10},{10,... | collective-permute-start | bytes 1572872 | tf_op jit(solution)/shard_map/ppermute | solution.py:265
  46.6 22.2 %copy-start.6 = (bf16[1280,256]{1,0:T(8,128)(2,1)S(1)}, bf16[1280,256]{1,0:T(8,128)(2,1)}, u32[]{:S(2)}) copy-start(bf16[1280,256]{1,0:T(8,128)(2,1)} %get-tuple-element.75.refs_0_) | copy-start | bytes 1966084
  46.6 22.2 %copy-start.7 = (bf16[1280,256]{1,0:T(8,128)(2,1)S(1)}, bf16[1280,256]{1,0:T(8,128)(2,1)}, u32[]{:S(2)}) copy-start(bf16[1280,256]{1,0:T(8,128)(2,1)} %get-tuple-element.76.refs_1_) | copy-start | bytes 1966084
  46.6 22.2 %copy-start.8 = (bf16[1280,256]{1,0:T(8,128)(2,1)S(1)}, bf16[1280,256]{1,0:T(8,128)(2,1)}, u32[]{:S(2)}) copy-start(bf16[1280,256]{1,0:T(8,128)(2,1)} %get-tuple-element.77.refs_2_) | copy-start | bytes 1966084
  68.8 34.8 %collective-permute-start.12 = (bf16[1280,256]{1,0:T(8,128)(2,1)S(1)}, bf16[1280,256]{1,0:T(8,128)(2,1)S(1)}, u32[]{:S(2)}, u32[]{:S(2)}) collective-permute-start(bf16[1280,256]{1,0:T(8,128)(2,1)S(1)} %get-tuple-element.97), channel_id=1, source_target_pairs={{0,1},{1,0},{2,3},{3,2},{4,5},{5,4},{6,7},{7,6},{8,9},{9,8},{10,11... | collective-permute-start | bytes 1966088 | tf_op jit(solution)/shard_map/ppermute | solution.py:265
  69.5 35.9 %collective-permute-start.13 = (bf16[1280,256]{1,0:T(8,128)(2,1)S(1)}, bf16[1280,256]{1,0:T(8,128)(2,1)S(1)}, u32[]{:S(2)}, u32[]{:S(2)}) collective-permute-start(bf16[1280,256]{1,0:T(8,128)(2,1)S(1)} %get-tuple-element.98), channel_id=1, source_target_pairs={{0,2},{1,3},{2,0},{3,1},{4,6},{5,7},{6,4},{7,5},{8,10},{9,11},{10,... | collective-permute-start | bytes 1966088 | tf_op jit(solution)/shard_map/ppermute | solution.py:265
  70.7 34.7 %collective-permute-start.14 = (bf16[1280,256]{1,0:T(8,128)(2,1)S(1)}, bf16[1280,256]{1,0:T(8,128)(2,1)S(1)}, u32[]{:S(2)}, u32[]{:S(2)}) collective-permute-start(bf16[1280,256]{1,0:T(8,128)(2,1)S(1)} %get-tuple-element.99), channel_id=1, source_target_pairs={{0,3},{1,2},{2,1},{3,0},{4,7},{5,6},{6,5},{7,4},{8,11},{9,10},{10,... | collective-permute-start | bytes 1966088 | tf_op jit(solution)/shard_map/ppermute | solution.py:265
  72.4 33.0 %copy-start.5 = (bf16[1280,256]{1,0:T(8,128)(2,1)S(1)}, bf16[1280,256]{1,0:T(8,128)(2,1)}, u32[]{:S(2)}) copy-start(bf16[1280,256]{1,0:T(8,128)(2,1)} %get-tuple-element.71.refs_5_.refs_7_) | copy-start | bytes 1966084
  101.8 40.3 %collective-permute-start.18 = (bf16[1792,256]{1,0:T(8,128)(2,1)S(1)}, bf16[1792,256]{1,0:T(8,128)(2,1)S(1)}, u32[]{:S(2)}, u32[]{:S(2)}) collective-permute-start(bf16[1792,256]{1,0:T(8,128)(2,1)S(1)} %get-tuple-element.111), channel_id=1, source_target_pairs={{0,1},{1,0},{2,3},{3,2},{4,5},{5,4},{6,7},{7,6},{8,9},{9,8},{10,11... | collective-permute-start | bytes 2752520 | tf_op jit(solution)/shard_map/ppermute | solution.py:265
  102.5 39.6 %collective-permute-start.19 = (bf16[1792,256]{1,0:T(8,128)(2,1)S(1)}, bf16[1792,256]{1,0:T(8,128)(2,1)S(1)}, u32[]{:S(2)}, u32[]{:S(2)}) collective-permute-start(bf16[1792,256]{1,0:T(8,128)(2,1)S(1)} %get-tuple-element.112), channel_id=1, source_target_pairs={{0,2},{1,3},{2,0},{3,1},{4,6},{5,7},{6,4},{7,5},{8,10},{9,11},{10,... | collective-permute-start | bytes 2752520 | tf_op jit(solution)/shard_map/ppermute | solution.py:265
  103.6 38.5 %collective-permute-start.20 = (bf16[1792,256]{1,0:T(8,128)(2,1)S(1)}, bf16[1792,256]{1,0:T(8,128)(2,1)S(1)}, u32[]{:S(2)}, u32[]{:S(2)}) collective-permute-start(bf16[1792,256]{1,0:T(8,128)(2,1)S(1)} %get-tuple-element.113), channel_id=1, source_target_pairs={{0,3},{1,2},{2,1},{3,0},{4,7},{5,6},{6,5},{7,4},{8,11},{9,10},{10,... | collective-permute-start | bytes 2752520 | tf_op jit(solution)/shard_map/ppermute | solution.py:265
  142.1 25.4 %copy-start.1 = (bf16[24,256,128]{2,1,0:T(8,128)(2,1)S(1)}, bf16[24,256,128]{2,1,0:T(8,128)(2,1)}, u32[]{:S(2)}) copy-start(bf16[24,256,128]{2,1,0:T(8,128)(2,1)} %param.11) | copy-start | bytes 4718596
  142.9 24.6 %copy-start = (bf16[24,256,128]{2,1,0:T(8,128)(2,1)S(1)}, bf16[24,256,128]{2,1,0:T(8,128)(2,1)}, u32[]{:S(2)}) copy-start(bf16[24,256,128]{2,1,0:T(8,128)(2,1)} %param.10) | copy-start | bytes 4718596
  142.9 2.7 %collective-permute-start.21 = (bf16[4,1024,128]{2,1,0:T(8,128)(2,1)S(1)}, bf16[4,1024,128]{2,1,0:T(8,128)(2,1)S(1)}, u32[]{:S(2)}, u32[]{:S(2)}) collective-permute-start(bf16[4,1024,128]{2,1,0:T(8,128)(2,1)S(1)} %hold.9), channel_id=1, source_target_pairs={{0,4},{4,0},{8,12},{12,8},{16,20},{20,16},{24,28},{28,24},{1,5},{5... | collective-permute-start | bytes 3145736 | tf_op jit(solution)/shard_map/ppermute | solution.py:268
  145.8 20.4 %collective-permute-start.24 = (bf16[1024,128]{1,0:T(8,128)(2,1)S(1)}, bf16[1024,128]{1,0:T(8,128)(2,1)S(1)}, u32[]{:S(2)}, u32[]{:S(2)}) collective-permute-start(bf16[1024,128]{1,0:T(8,128)(2,1)S(1)} %get-tuple-element.126), channel_id=1, source_target_pairs={{0,24},{4,28},{8,16},{12,20},{16,8},{20,12},{24,0},{28,4},{1,25},{... | collective-permute-start | bytes 786440 | tf_op jit(solution)/shard_map/ppermute | solution.py:445
  146.4 26.0 %collective-permute-start.23 = (bf16[1024,128]{1,0:T(8,128)(2,1)S(1)}, bf16[1024,128]{1,0:T(8,128)(2,1)S(1)}, u32[]{:S(2)}, u32[]{:S(2)}) collective-permute-start(bf16[1024,128]{1,0:T(8,128)(2,1)S(1)} %get-tuple-element.127), channel_id=1, source_target_pairs={{0,16},{4,20},{8,24},{12,28},{16,0},{20,4},{24,8},{28,12},{1,17},{... | collective-permute-start | bytes 786440 | tf_op jit(solution)/shard_map/ppermute | solution.py:445
  149.8 22.6 %collective-permute-start.22 = (bf16[1024,128]{1,0:T(8,128)(2,1)S(1)}, bf16[1024,128]{1,0:T(8,128)(2,1)S(1)}, u32[]{:S(2)}, u32[]{:S(2)}) collective-permute-start(bf16[1024,128]{1,0:T(8,128)(2,1)S(1)} %get-tuple-element.125), channel_id=1, source_target_pairs={{0,8},{4,12},{8,0},{12,4},{16,24},{20,28},{24,16},{28,20},{1,9},{5... | collective-permute-start | bytes 786440 | tf_op jit(solution)/shard_map/ppermute | solution.py:445
  149.8 28.4 %collective-permute-start.15 = (bf16[1280,256]{1,0:T(8,128)(2,1)}, bf16[1280,256]{1,0:T(8,128)(2,1)}, u32[]{:S(2)}, u32[]{:S(2)}) collective-permute-start(bf16[1280,256]{1,0:T(8,128)(2,1)} %get-tuple-element.107), channel_id=1, source_target_pairs={{0,1},{1,0},{2,3},{3,2},{4,5},{5,4},{6,7},{7,6},{8,9},{9,8},{10,11... | collective-permute-start | bytes 1966088 | tf_op jit(solution)/shard_map/ppermute | solution.py:265
  150.4 27.8 %collective-permute-start.16 = (bf16[1280,256]{1,0:T(8,128)(2,1)}, bf16[1280,256]{1,0:T(8,128)(2,1)}, u32[]{:S(2)}, u32[]{:S(2)}) collective-permute-start(bf16[1280,256]{1,0:T(8,128)(2,1)} %get-tuple-element.108), channel_id=1, source_target_pairs={{0,2},{1,3},{2,0},{3,1},{4,6},{5,7},{6,4},{7,5},{8,10},{9,11},{10,... | collective-permute-start | bytes 1966088 | tf_op jit(solution)/shard_map/ppermute | solution.py:265
  166.3 17.9 %collective-permute-start.17 = (bf16[1280,256]{1,0:T(8,128)(2,1)}, bf16[1280,256]{1,0:T(8,128)(2,1)}, u32[]{:S(2)}, u32[]{:S(2)}) collective-permute-start(bf16[1280,256]{1,0:T(8,128)(2,1)} %get-tuple-element.109), channel_id=1, source_target_pairs={{0,3},{1,2},{2,1},{3,0},{4,7},{5,6},{6,5},{7,4},{8,11},{9,10},{10,... | collective-permute-start | bytes 1966088 | tf_op jit(solution)/shard_map/ppermute | solution.py:265
  174.1 15.0 %all-to-all-start = ((bf16[4,256,128]{1,2,0:T(8,128)(2,1)}), bf16[4,256,128]{1,2,0:T(8,128)(2,1)S(1)}, u32[]{:S(2)}, u32[]{:S(2)}) async-start(bf16[4,256,128]{1,2,0:T(8,128)(2,1)} %copy.37), calls=%async_computation | async-start | bytes 524288 | tf_op jit(solution)/shard_map/all_to_all | solution.py:447
  (13 other events, 100.5 us)
